TPU v7x, 512 devices: a whole 4x4x16 slice. The times are simulated.
512 devices in a mesh: ctx: 32 (over x_hi, z), tp: 16 (over y, x_lo, core).
Axes of the slice: x: 4 (x_hi: 2, x_lo: 2; x = x_hi * 2 + x_lo), y: 4, z: 16, core: 2. Of those that a mesh axis runs over, the one named last changes fastest.
Arguments:
- queries: bfloat16 [16384, 4096], P('ctx', 'tp'), may hold values from -12 to 12
- keys: bfloat16 [16384, 512], P('ctx'), may hold values from -5 to 5
- values: bfloat16 [16384, 512], P('ctx'), may hold values from -6 to 6
- out_grad: bfloat16 [16384, 4096], P('ctx', 'tp'), may hold values from -6 to 6
- doc_lengths: int32 [32], replicated, may hold values from 1 to 2048, 16384 in all
Outputs:
- attn_out: bfloat16 [16384, 4096], P('ctx', 'tp')
- query_grad: bfloat16 [16384, 4096], P('ctx', 'tp')
- key_grad: bfloat16 [16384, 512], P('ctx')
- value_grad: bfloat16 [16384, 512], P('ctx')
Inputs may be any that keep to these rules, and one draw needn't show every extreme that they name: `doc_lengths`: the lengths sum to 16384; the largest is exactly 2048.
All inputs are finite; a program needn't handle non-finite values.
Results may differ from a plain program's by a relative error of at most 0.025.
Values may be sent and summed in bfloat16 or wider, within the bound.
A program may use at most 128 MiB of HBM per device.

v0:
```python
import math

import jax
import jax.numpy as jnp
from jax import lax
from jax.sharding import PartitionSpec as P

H = 32
KVH = 4
REACH = 4


NEG = -1e30


def from_behind(value, axis, steps):
    count = lax.axis_size(axis)
    initial, last = (max(0, -steps), min(count, count - steps))
    return lax.ppermute(value, axis, [(source, source + steps) for source in range(initial, last)])


def doc_index(positions, ends):
    return jnp.sum((positions[:, None] >= ends[None, :]).astype(jnp.int32), axis=1)


def tile_mask(qpos, qdoc, kpos, kdoc, total):
    same = qdoc[:, None] == kdoc[None, :]
    causal = kpos[None, :] <= qpos[:, None]
    inside = (kpos[None, :] >= 0) & (qpos[:, None] < total)
    return same & causal & inside


def tile_scores(qheads, key_tile, scale):
    return jnp.einsum("qhd,kd->hqk", qheads, key_tile, preferred_element_type=jnp.float32) * scale


def guarded(live, operands):
    return live(*operands)


def grad_tile(qheads, grad_heads, key_tile, val_tile, mask, lse, delta, scale):
    scores = tile_scores(qheads, key_tile, scale)
    probs = jnp.where(mask[None], jnp.exp(scores - lse[:, :, None]), 0.0)
    probs_b = probs.astype(jnp.bfloat16)
    dprob = jnp.einsum("qhd,kd->hqk", grad_heads, val_tile, preferred_element_type=jnp.float32)
    dscore = (probs * (dprob - delta[:, :, None])).astype(jnp.bfloat16)
    return (probs_b, dscore)


def key_side(qheads, grad_heads, probs_b, dscore, scale):
    kgrad = jnp.einsum("hqk,qhd->kd", dscore, qheads, preferred_element_type=jnp.float32) * scale
    vgrad = jnp.einsum("hqk,qhd->kd", probs_b, grad_heads, preferred_element_type=jnp.float32)
    return jnp.concatenate([kgrad, vgrad], axis=1)


def per_device(queries, keys, values, out_grad, doc_lengths):
    blk = queries.shape[0]
    head_dim = keys.shape[1] // KVH
    heads_here = queries.shape[1] // head_dim
    scale = 1.0 / math.sqrt(head_dim)
    ctx_idx = lax.axis_index("ctx")
    n_ctx = lax.axis_size("ctx")
    tp_idx = lax.axis_index("tp")
    total = n_ctx * blk
    kv_head = tp_idx * heads_here // (H // KVH)
    own_keys = lax.dynamic_slice_in_dim(keys, kv_head * head_dim, head_dim, 1)
    own_vals = lax.dynamic_slice_in_dim(values, kv_head * head_dim, head_dim, 1)
    pair = jnp.concatenate([own_keys, own_vals], axis=1)
    ends = jnp.cumsum(doc_lengths)
    offsets = jnp.arange(blk, dtype=jnp.int32)

    def block_rows(index):
        positions = index * blk + offsets
        return (positions, doc_index(positions, ends))

    qpos, qdoc = block_rows(ctx_idx)
    qheads = queries.reshape(blk, heads_here, head_dim)
    grad_heads = out_grad.reshape(blk, heads_here, head_dim)
    tiles = [pair]
    for step in range(1, REACH + 1):
        tiles.append(from_behind(pair, "ctx", step))
    masks = []
    for step in range(REACH + 1):
        kpos, kdoc = block_rows(ctx_idx - step)
        masks.append(tile_mask(qpos, qdoc, kpos, kdoc, total))

    def stats_live(tile, mask, run_max, run_sum):
        scores = tile_scores(qheads, tile[:, :head_dim], scale)
        top = jnp.max(jnp.where(mask[None], scores, NEG), axis=2)
        new_max = jnp.maximum(run_max, top)
        fresh = jnp.sum(jnp.where(mask[None], jnp.exp(scores - new_max[:, :, None]), 0.0), axis=2)
        return (new_max, run_sum * jnp.exp(run_max - new_max) + fresh, scores)

    run_max = jnp.full((heads_here, blk), NEG, jnp.float32)
    run_sum = jnp.zeros((heads_here, blk), jnp.float32)
    kept_scores = []
    for step in range(REACH + 1):
        run_max, run_sum, scores = guarded(stats_live, (tiles[step], masks[step], run_max, run_sum))
        kept_scores.append(scores)
    lse = run_max + jnp.log(run_sum)

    def out_live(scores, tile, mask, acc):
        probs_b = jnp.where(mask[None], jnp.exp(scores - lse[:, :, None]), 0.0).astype(jnp.bfloat16)
        return acc + jnp.einsum(
            "hqk,kd->qhd", probs_b, tile[:, head_dim:], preferred_element_type=jnp.float32
        )

    acc = jnp.zeros((blk, heads_here, head_dim), jnp.float32)
    for step in range(REACH + 1):
        acc = guarded(out_live, (kept_scores[step], tiles[step], masks[step], acc))
    attn = acc.astype(jnp.bfloat16)
    delta = jnp.sum(grad_heads.astype(jnp.float32) * attn.astype(jnp.float32), axis=2).T

    def make_back():

        def back_live(tile, mask, qgrad):
            probs_b, dscore = grad_tile(
                qheads, grad_heads, tile[:, :head_dim], tile[:, head_dim:], mask, lse, delta, scale
            )
            qgrad = (
                qgrad
                + jnp.einsum(
                    "hqk,kd->qhd", dscore, tile[:, :head_dim], preferred_element_type=jnp.float32
                )
                * scale
            )
            return (qgrad, key_side(qheads, grad_heads, probs_b, dscore, scale))

        return back_live

    qgrad = jnp.zeros((blk, heads_here, head_dim), jnp.float32)
    terms = []
    for step in range(REACH + 1):
        qgrad, term = guarded(make_back(), (tiles[step], masks[step], qgrad))
        terms.append(term)
    own = terms[0]
    for step in range(1, REACH + 1):
        own = own + from_behind(terms[step].astype(jnp.bfloat16), "ctx", -step).astype(jnp.float32)
    placed_keys = lax.dynamic_update_slice_in_dim(
        jnp.zeros((blk, KVH * head_dim), jnp.float32), own[:, :head_dim], kv_head * head_dim, 1
    )
    placed_vals = lax.dynamic_update_slice_in_dim(
        jnp.zeros((blk, KVH * head_dim), jnp.float32), own[:, head_dim:], kv_head * head_dim, 1
    )
    key_sum, val_sum = lax.psum((placed_keys, placed_vals), "tp")
    key_full = key_sum.astype(jnp.bfloat16)
    val_full = val_sum.astype(jnp.bfloat16)
    attn_out = attn.reshape(blk, heads_here * head_dim)
    query_grad = qgrad.astype(jnp.bfloat16).reshape(blk, heads_here * head_dim)
    return (attn_out, query_grad, key_full, val_full)


def solution(mesh):
    placed = (P("ctx", "tp"), P("ctx", None), P("ctx", None), P("ctx", "tp"), P())
    return jax.shard_map(
        per_device,
        mesh=mesh,
        in_specs=placed,
        out_specs=(P("ctx", "tp"), P("ctx", "tp"), P("ctx", None), P("ctx", None)),
        check_vma=False,
    )
```

profile of v0, /device:TPU:4, one launch (start us, length us, event | category | flops | bytes accessed | tf_op | source)
XLA Modules:
  0.0 223.7 jit_solution(16142071274522583184)
XLA Ops:
  0.7 1.0 constant_dynamic-slice_fusion
  1.7 6.5 %collective-permute-start.2 = (bf16[512,256]{1,0:T(8,128)(2,1)S(1)}, bf16[512,256]{1,0:T(8,128)(2,1)S(1)}, u32[]{:S(2)}, u32[]{:S(2)}) collective-permute-start(bf16[512,256]{1,0:T(8,128)(2,1)S(1)} %pad_maximum_fusion), channel_id=1, source_target_pairs={{0,48},{16,64},{32,80},{48,96},{64,112},{80,128},{96,144},{112,160... | collective-permute-start | bytes 786440 | tf_op jit(solution)/shard_map/ppermute | solution.py:19
  8.2 6.4 %collective-permute-start.1 = (bf16[512,256]{1,0:T(8,128)(2,1)S(1)}, bf16[512,256]{1,0:T(8,128)(2,1)S(1)}, u32[]{:S(2)}, u32[]{:S(2)}) collective-permute-start(bf16[512,256]{1,0:T(8,128)(2,1)S(1)} %pad_maximum_fusion), channel_id=1, source_target_pairs={{0,32},{16,48},{32,64},{48,80},{64,96},{80,112},{96,128},{112,144}... | collective-permute-start | bytes 786440 | tf_op jit(solution)/shard_map/ppermute | solution.py:19
  14.6 3.8 %collective-permute-start = (bf16[512,256]{1,0:T(8,128)(2,1)S(1)}, bf16[512,256]{1,0:T(8,128)(2,1)S(1)}, u32[]{:S(2)}, u32[]{:S(2)}) collective-permute-start(bf16[512,256]{1,0:T(8,128)(2,1)S(1)} %pad_maximum_fusion), channel_id=1, source_target_pairs={{0,16},{16,32},{32,48},{48,64},{64,80},{80,96},{96,112},{112,128},... | collective-permute-start | bytes 786440 | tf_op jit(solution)/shard_map/ppermute | solution.py:19
  18.5 7.3 %collective-permute-start.3 = (bf16[512,256]{1,0:T(8,128)(2,1)S(1)}, bf16[512,256]{1,0:T(8,128)(2,1)S(1)}, u32[]{:S(2)}, u32[]{:S(2)}) collective-permute-start(bf16[512,256]{1,0:T(8,128)(2,1)S(1)} %pad_maximum_fusion), channel_id=1, source_target_pairs={{0,64},{16,80},{32,96},{48,112},{64,128},{80,144},{96,160},{112,17... | collective-permute-start | bytes 786440 | tf_op jit(solution)/shard_map/ppermute | solution.py:19
  26.8 1.1 copy.207
  27.9 1.1 copy.127
  29.1 1.8 and_and_fusion.4
  32.0 10.1 %collective-permute-done.1 = bf16[512,256]{1,0:T(8,128)(2,1)S(1)} collective-permute-done((bf16[512,256]{1,0:T(8,128)(2,1)S(1)}, bf16[512,256]{1,0:T(8,128)(2,1)S(1)}, u32[]{:S(2)}, u32[]{:S(2)}) %collective-permute-start.1) | collective-permute-done | bytes 262176 | tf_op jit(solution)/shard_map/ppermute | solution.py:19
  42.6 9.0 %collective-permute-done = bf16[512,256]{1,0:T(8,128)(2,1)S(1)} collective-permute-done((bf16[512,256]{1,0:T(8,128)(2,1)S(1)}, bf16[512,256]{1,0:T(8,128)(2,1)S(1)}, u32[]{:S(2)}, u32[]{:S(2)}) %collective-permute-start) | collective-permute-done | bytes 262176 | tf_op jit(solution)/shard_map/ppermute | solution.py:19
  52.2 7.9 %collective-permute-done.3 = bf16[512,256]{1,0:T(8,128)(2,1)S(1)} collective-permute-done((bf16[512,256]{1,0:T(8,128)(2,1)S(1)}, bf16[512,256]{1,0:T(8,128)(2,1)S(1)}, u32[]{:S(2)}, u32[]{:S(2)}) %collective-permute-start.3) | collective-permute-done | bytes 262176 | tf_op jit(solution)/shard_map/ppermute | solution.py:19
  66.7 1.4 convolution_bitcast_fusion.8
  71.8 1.0 fusion.7
  73.3 17.0 %collective-permute-start.4 = (bf16[512,256]{0,1:T(8,128)(2,1)S(1)}, bf16[512,256]{0,1:T(8,128)(2,1)}, u32[]{:S(2)}, u32[]{:S(2)}) collective-permute-start(bf16[512,256]{0,1:T(8,128)(2,1)S(1)} %pad_maximum_fusion.1), channel_id=1, source_target_pairs={{16,0},{32,16},{48,32},{64,48},{80,64},{96,80},{112,96},{128,112},... | collective-permute-start | bytes 786440 | tf_op jit(solution)/shard_map/ppermute | solution.py:19
  91.6 2.1 collective-permute-start.5
  95.0 5.4 %collective-permute-start.6 = (bf16[512,256]{0,1:T(8,128)(2,1)S(1)}, bf16[512,256]{0,1:T(8,128)(2,1)}, u32[]{:S(2)}, u32[]{:S(2)}) collective-permute-start(bf16[512,256]{0,1:T(8,128)(2,1)S(1)} %pad_maximum_fusion.3), channel_id=1, source_target_pairs={{48,0},{64,16},{80,32},{96,48},{112,64},{128,80},{144,96},{160,112... | collective-permute-start | bytes 786440 | tf_op jit(solution)/shard_map/ppermute | solution.py:19
  102.4 2.4 %collective-permute-start.7 = (bf16[512,256]{0,1:T(8,128)(2,1)}, bf16[512,256]{0,1:T(8,128)(2,1)}, u32[]{:S(2)}, u32[]{:S(2)}) collective-permute-start(bf16[512,256]{0,1:T(8,128)(2,1)} %pad_maximum_fusion.4), channel_id=1, source_target_pairs={{64,0},{80,16},{96,32},{112,48},{128,64},{144,80},{160,96},{176,11... | collective-permute-start | bytes 786440 | tf_op jit(solution)/shard_map/ppermute | solution.py:19
  106.6 0.8 copy.161
  107.4 0.8 copy.160
  108.7 1.9 collective-permute-done.5
  110.7 31.3 %collective-permute-done.6 = bf16[512,256]{0,1:T(8,128)(2,1)} collective-permute-done((bf16[512,256]{0,1:T(8,128)(2,1)S(1)}, bf16[512,256]{0,1:T(8,128)(2,1)}, u32[]{:S(2)}, u32[]{:S(2)}) %collective-permute-start.6) | collective-permute-done | bytes 262176 | tf_op jit(solution)/shard_map/ppermute | solution.py:19
  142.0 5.5 %collective-permute-done.7 = bf16[512,256]{0,1:T(8,128)(2,1)} collective-permute-done((bf16[512,256]{0,1:T(8,128)(2,1)}, bf16[512,256]{0,1:T(8,128)(2,1)}, u32[]{:S(2)}, u32[]{:S(2)}) %collective-permute-start.7) | collective-permute-done | bytes 262176 | tf_op jit(solution)/shard_map/ppermute | solution.py:19
  147.4 1.4 fusion.67
  149.4 74.3 %all-reduce.2 = (bf16[512,512]{1,0:T(8,128)(2,1)}, bf16[512,512]{1,0:T(8,128)(2,1)}) all-reduce(f32[512,512]{1,0:T(8,128)S(1)} %constant_dynamic-update-slice_fusion.1, f32[512,512]{1,0:T(8,128)S(1)} %constant_dynamic-update-slice_fusion), channel_id=1, replica_groups=mesh['ctx'=32,'tp'=16] {'tp'}, use_global_device_ids=true, to_apply=%region_17.18 | all-reduce | flops 524288 | bytes 3145728 | tf_op jit(solution)/shard_map/psum | solution.py:145
  (69 shorter events, 21.3 us)
Async XLA Ops:
  1.7 29.8 %collective-permute-start.2 = (bf16[512,256]{1,0:T(8,128)(2,1)S(1)}, bf16[512,256]{1,0:T(8,128)(2,1)S(1)}, u32[]{:S(2)}, u32[]{:S(2)}) collective-permute-start(bf16[512,256]{1,0:T(8,128)(2,1)S(1)} %pad_maximum_fusion), channel_id=1, source_target_pairs={{0,48},{16,64},{32,80},{48,96},{64,112},{80,128},{96,144},{112,160... | collective-permute-start | bytes 786440 | tf_op jit(solution)/shard_map/ppermute | solution.py:19
  8.2 33.9 %collective-permute-start.1 = (bf16[512,256]{1,0:T(8,128)(2,1)S(1)}, bf16[512,256]{1,0:T(8,128)(2,1)S(1)}, u32[]{:S(2)}, u32[]{:S(2)}) collective-permute-start(bf16[512,256]{1,0:T(8,128)(2,1)S(1)} %pad_maximum_fusion), channel_id=1, source_target_pairs={{0,32},{16,48},{32,64},{48,80},{64,96},{80,112},{96,128},{112,144}... | collective-permute-start | bytes 786440 | tf_op jit(solution)/shard_map/ppermute | solution.py:19
  14.6 37.0 %collective-permute-start = (bf16[512,256]{1,0:T(8,128)(2,1)S(1)}, bf16[512,256]{1,0:T(8,128)(2,1)S(1)}, u32[]{:S(2)}, u32[]{:S(2)}) collective-permute-start(bf16[512,256]{1,0:T(8,128)(2,1)S(1)} %pad_maximum_fusion), channel_id=1, source_target_pairs={{0,16},{16,32},{32,48},{48,64},{64,80},{80,96},{96,112},{112,128},... | collective-permute-start | bytes 786440 | tf_op jit(solution)/shard_map/ppermute | solution.py:19
  18.5 41.6 %collective-permute-start.3 = (bf16[512,256]{1,0:T(8,128)(2,1)S(1)}, bf16[512,256]{1,0:T(8,128)(2,1)S(1)}, u32[]{:S(2)}, u32[]{:S(2)}) collective-permute-start(bf16[512,256]{1,0:T(8,128)(2,1)S(1)} %pad_maximum_fusion), channel_id=1, source_target_pairs={{0,64},{16,80},{32,96},{48,112},{64,128},{80,144},{96,160},{112,17... | collective-permute-start | bytes 786440 | tf_op jit(solution)/shard_map/ppermute | solution.py:19
  31.5 62.2 %copy-start.1 = (bf16[512,256]{1,0:T(8,128)(2,1)}, bf16[512,256]{1,0:T(8,128)(2,1)S(1)}, u32[]{:S(2)}) copy-start(bf16[512,256]{1,0:T(8,128)(2,1)S(1)} %collective-permute-done.2) | copy-start | bytes 786436
  60.1 8.7 %copy-start.3 = (bf16[512,256]{1,0:T(8,128)(2,1)}, bf16[512,256]{1,0:T(8,128)(2,1)S(1)}, u32[]{:S(2)}) copy-start(bf16[512,256]{1,0:T(8,128)(2,1)S(1)} %collective-permute-done.3) | copy-start | bytes 786436
  73.3 35.5 %collective-permute-start.4 = (bf16[512,256]{0,1:T(8,128)(2,1)S(1)}, bf16[512,256]{0,1:T(8,128)(2,1)}, u32[]{:S(2)}, u32[]{:S(2)}) collective-permute-start(bf16[512,256]{0,1:T(8,128)(2,1)S(1)} %pad_maximum_fusion.1), channel_id=1, source_target_pairs={{16,0},{32,16},{48,32},{64,48},{80,64},{96,80},{112,96},{128,112},... | collective-permute-start | bytes 786440 | tf_op jit(solution)/shard_map/ppermute | solution.py:19
  91.6 8.8 %copy-start.4 = (bf16[512,256]{1,0:T(8,128)(2,1)S(1)}, bf16[512,256]{1,0:T(8,128)(2,1)}, u32[]{:S(2)}) copy-start(bf16[512,256]{1,0:T(8,128)(2,1)} %copy-done.3) | copy-start | bytes 786436
  91.6 19.1 %collective-permute-start.5 = (bf16[512,256]{0,1:T(8,128)(2,1)S(1)}, bf16[512,256]{0,1:T(8,128)(2,1)}, u32[]{:S(2)}, u32[]{:S(2)}) collective-permute-start(bf16[512,256]{0,1:T(8,128)(2,1)S(1)} %pad_maximum_fusion.2), channel_id=1, source_target_pairs={{32,0},{48,16},{64,32},{80,48},{96,64},{112,80},{128,96},{144,112}... | collective-permute-start | bytes 786440 | tf_op jit(solution)/shard_map/ppermute | solution.py:19
  95.0 47.0 %collective-permute-start.6 = (bf16[512,256]{0,1:T(8,128)(2,1)S(1)}, bf16[512,256]{0,1:T(8,128)(2,1)}, u32[]{:S(2)}, u32[]{:S(2)}) collective-permute-start(bf16[512,256]{0,1:T(8,128)(2,1)S(1)} %pad_maximum_fusion.3), channel_id=1, source_target_pairs={{48,0},{64,16},{80,32},{96,48},{112,64},{128,80},{144,96},{160,112... | collective-permute-start | bytes 786440 | tf_op jit(solution)/shard_map/ppermute | solution.py:19
  101.2 4.0 %copy-start.2 = (bf16[512,256]{1,0:T(8,128)(2,1)S(1)}, bf16[512,256]{1,0:T(8,128)(2,1)}, u32[]{:S(2)}) copy-start(bf16[512,256]{1,0:T(8,128)(2,1)} %copy-done.1) | copy-start | bytes 786436
  102.4 45.0 %collective-permute-start.7 = (bf16[512,256]{0,1:T(8,128)(2,1)}, bf16[512,256]{0,1:T(8,128)(2,1)}, u32[]{:S(2)}, u32[]{:S(2)}) collective-permute-start(bf16[512,256]{0,1:T(8,128)(2,1)} %pad_maximum_fusion.4), channel_id=1, source_target_pairs={{64,0},{80,16},{96,32},{112,48},{128,64},{144,80},{160,96},{176,11... | collective-permute-start | bytes 786440 | tf_op jit(solution)/shard_map/ppermute | solution.py:19
  106.2 41.2 %copy-start = (f32[512,128]{0,1:T(8,128)S(1)}, f32[512,128]{0,1:T(8,128)}, u32[]{:S(2)}) copy-start(f32[512,128]{0,1:T(8,128)} %convolution_bitcast_fusion.8) | copy-start | bytes 786436
where the time goes:
time: 224 us
  blocking collectives  74.3 us (33%)
  waiting for transfers between devices  65.7 us (29%)
  starting transfers between devices  50.9 us (23%)
  matrix products  18.6 us (8%)
  other arithmetic  6.85 us (3%)
  local copies, waits for them, and re-layouts  6.21 us (3%)
    psum x1, blocking collectives, per_device(): key_sum, val_sum = lax.psum((placed_keys, placed_vals), 'tp')  74.3 us
    ppermute x8, waiting for transfers between devices, from_behind(): lax.ppermute(value, axis, [(source, source + steps) for source in range(i...  65.7 us
    ppermute x8, starting transfers between devices, from_behind(): lax.ppermute(value, axis, [(source, source + steps) for source in range(i...  50.9 us
  transfers between devices with their start and end apart: 8, of which 6 were waited for; matrix products, arithmetic and copies ran while one was open for 7% of the time, Pallas kernels for 0%

commit v1 on v0

v1 whole, which is shorter than its diff:
```python
import functools
import math

import jax
import jax.numpy as jnp
from jax import lax
from jax.experimental import pallas as pl
from jax.experimental.pallas import tpu as pltpu
from jax.sharding import PartitionSpec as P

MESH = pl.DeviceIdType.MESH
HD = 128
KVH = 4
REACH = 4
BLK = 512
QN = 1024
CH = 256
QUART = 128
NSUB = 2
SUB = QUART // NSUB
STRAIGHT = (3, 4)
NEG = -1e30
FLOOR = -1e9
SCALE = 1.0 / math.sqrt(HD)
EXPC = SCALE * math.log2(math.e)
F32 = jnp.float32
BF = jnp.bfloat16


def nt(a, b):
    return lax.dot_general(a, b, (((1,), (1,)), ((), ())), preferred_element_type=F32)


def nn(a, b):
    return jnp.dot(a, b, preferred_element_type=F32)


def kernel(n_ctx, ndoc, q_hbm, k_hbm, v_hbm, g_hbm, len_ref, o_ref, dq_ref, dk_ref, dv_ref,
           q_in, g_in, kv, qt, gt, kvt, probs, dprob, acc, ot, dqt, gs, qs, ds,
           term, cbuf, dbuf, hold, xsend, xbuf, zbuf, zsend, lsem, ssem, rsem):
    c = lax.axis_index("ctx")
    t = lax.axis_index("tp")
    half_ctx = n_ctx // 2
    y, xlo, core = t // 4, (t // 2) % 2, t % 2
    xhi = c // half_ctx
    xl = xlo + xhi - 2 * xlo * xhi

    def place(ctx, yy, xx, cc):
        hi = ctx // half_ctx
        lo = xx + hi - 2 * xx * hi
        return (ctx, yy * 4 + lo * 2 + cc)

    z_next = place((c + 1) % n_ctx, y, xl, core)
    z_prev = place((c + n_ctx - 1) % n_ctx, y, xl, core)
    x_peer = place(c, y, 1 - xl, core)
    c_peer = place(c, y, xl, 1 - core)
    y_next = place(c, (y + 1) % 4, xl, core)
    y_prev = place(c, (y + 3) % 4, xl, core)
    x_diag = place(c, y, 1 - xl, 1 - core)
    y_next_o = place(c, (y + 1) % 4, xl, 1 - core)
    y_prev_o = place(c, (y + 3) % 4, xl, 1 - core)

    col = pl.ds(pl.multiple_of(y * HD, HD), HD)
    my_half = pl.multiple_of(core * 256, 256)
    my_rows = pl.ds(pl.multiple_of(core * 256 + xl * QUART, QUART), QUART)
    sub_rows = [pl.ds(pl.multiple_of(core * 256 + xl * QUART + k * SUB, SUB), SUB) for k in range(NSUB)]
    half_rows = pl.ds(my_half, 256)
    peer_half = pl.ds(pl.multiple_of((1 - core) * 256, 256), 256)

    loads = [
        pltpu.make_async_copy(q_hbm, q_in, lsem.at[0]),
        pltpu.make_async_copy(g_hbm, g_in, lsem.at[1]),
        pltpu.make_async_copy(k_hbm.at[:, col], kv.at[0, 0], lsem.at[2]),
        pltpu.make_async_copy(v_hbm.at[:, col], kv.at[0, 1], lsem.at[3]),
    ]
    for cp in loads:
        cp.start()

    barrier = pltpu.get_barrier_semaphore()
    peers = (z_next, z_prev, x_peer, c_peer, y_next, y_prev, x_diag, y_next_o, y_prev_o)
    for dev in peers:
        pl.semaphore_signal(barrier, inc=1, device_id=dev, device_id_type=MESH)
    pl.semaphore_wait(barrier, len(peers))

    sent = []

    def send(src, dst, dev):
        i = len(sent)
        cp = pltpu.make_async_remote_copy(src_ref=src, dst_ref=dst, send_sem=ssem.at[i], recv_sem=rsem.at[i],
                                          device_id=dev, device_id_type=MESH)
        cp.start()
        sent.append(cp)
        return cp

    zc, xc, cc, dc = {}, {}, {}, {}
    for j, src in ((0, k_hbm), (1, v_hbm)):
        for k in range(NSUB):
            zc[1, j, k] = send(src.at[sub_rows[k], col], kv.at[1, j, sub_rows[k]], z_next)

    lane = lax.broadcasted_iota(jnp.int32, (1, BLK), 1)
    pos = lane + c * BLK
    start = jnp.zeros((1, BLK), jnp.int32)
    end = jnp.int32(0)
    for d in range(ndoc):
        end = end + len_ref[d]
        start = jnp.where(pos >= end, end, start)
    krow = lax.broadcasted_iota(jnp.int32, (BLK, CH), 0)

    for cp in loads:
        cp.wait()
    for h in range(2):
        qt[:, h * BLK:(h + 1) * BLK] = q_in[:, h * HD:(h + 1) * HD].T
        gt[:, h * BLK:(h + 1) * BLK] = g_in[:, h * HD:(h + 1) * HD].T

    nch = QN // CH
    m_run = [jnp.full((1, CH), FLOOR, F32)] * nch
    l_run = [jnp.zeros((1, CH), F32)] * nch
    m_at = {}

    def forward(s):
        keys, vals = kv[s, 0], kv[s, 1]
        kvt[s, 0] = keys.T
        vt = vals.T
        for i in range(nch):
            lo = i * CH
            off = (i * CH) % BLK
            sc = nn(keys, qt[:, lo:lo + CH])
            first = start[:, off:off + CH] - (c - s) * BLK
            seen = krow >= first
            if s == 0:
                seen = seen & (krow <= lane[:, off:off + CH])
            sc = jnp.where(seen, sc, NEG)
            top = jnp.maximum(m_run[i], jnp.max(sc, axis=0, keepdims=True))
            p = jnp.exp2(sc * EXPC - top * EXPC)
            fade = jnp.exp2((m_run[i] - top) * EXPC)
            l_run[i] = l_run[i] * fade + jnp.sum(p, axis=0, keepdims=True)
            m_run[i] = top
            m_at[s, i] = top
            pb = p.astype(BF)
            probs[s, :, lo:lo + CH] = pb
            part = nn(vt, pb)
            if s == 0:
                acc[:, lo:lo + CH] = part
            else:
                acc[:, lo:lo + CH] = acc[:, lo:lo + CH] * fade + part
            dprob[s, :, lo:lo + CH] = nn(vals, gt[:, lo:lo + CH])

    def take_z(s):
        for j in range(2):
            for k in range(NSUB):
                zc[s, j, k].wait_recv()
                if s < REACH:
                    zc[s + 1, j, k] = send(kv.at[s, j, sub_rows[k]], kv.at[s + 1, j, sub_rows[k]], z_next)
            piece = kv.at[s, j, my_rows]
            xc[s, j] = send(piece, piece, x_peer)
            if s == REACH:
                dc[s, j] = send(piece, piece, x_diag)
                cc[s, j] = send(piece, piece, c_peer)

    def take_x(s):
        for j in range(2):
            xc[s, j].wait_recv()
            if s < REACH:
                cc[s, j] = send(kv.at[s, j, half_rows], kv.at[s, j, half_rows], c_peer)

    def take_c(s):
        for j in range(2):
            cc[s, j].wait_recv()
            if s == REACH:
                dc[s, j].wait_recv()

    take_z(1)
    for s in range(1, REACH + 1):
        if s < REACH:
            take_z(s + 1)
            take_x(s)
        if s > 1:
            take_c(s - 1)
        forward(s - 1)
    take_x(REACH)
    take_c(REACH)
    forward(REACH)

    inv, delta = [], []
    for i in range(nch):
        inv.append(1.0 / l_run[i])

    def finish():
        for i in range(nch):
            lo = i * CH
            out = (acc[:, lo:lo + CH] * inv[i]).astype(BF)
            ot[:, lo:lo + CH] = out
            delta.append(jnp.sum(gt[:, lo:lo + CH].astype(F32) * out.astype(F32), axis=0, keepdims=True))

    bc, bx, bz = {}, {}, {}
    far_x = pl.ds(pl.multiple_of(core * 256 + (1 - xl) * QUART, QUART), QUART)
    far_c = pl.ds(pl.multiple_of((1 - core) * 256 + xl * QUART, QUART), QUART)
    far_d = pl.ds(pl.multiple_of((1 - core) * 256 + (1 - xl) * QUART, QUART), QUART)

    def give(s, j):
        if s in STRAIGHT:
            bx[s, j] = [send(term.at[s, j, rows], dbuf.at[s - STRAIGHT[0], j, i], dev)
                        for i, (rows, dev) in enumerate(((far_x, x_peer), (far_d, x_diag), (far_c, c_peer)))]
        else:
            bc[s, j] = send(term.at[s, j, peer_half], cbuf.at[s, j], c_peer)

    def backward(s):
        b = s % 2
        fac = [jnp.exp2((m_at[s, i] - m_run[i]) * EXPC) * inv[i] for i in range(nch)]
        for i in range(nch):
            lo = i * CH
            gs[b, :, lo:lo + CH] = (gt[:, lo:lo + CH].astype(F32) * fac[i]).astype(BF)
            qs[b, :, lo:lo + CH] = (qt[:, lo:lo + CH].astype(F32) * (fac[i] * SCALE)).astype(BF)
        term[s, 1] = nt(probs[s], gs[b]).astype(BF)
        give(s, 1)
        if s == REACH:
            finish()
        for i in range(nch):
            lo = i * CH
            dsc = (probs[s, :, lo:lo + CH].astype(F32) * (dprob[s, :, lo:lo + CH] - delta[i])).astype(BF)
            ds[b, :, lo:lo + CH] = dsc
            part = nn(kvt[s, 0], dsc) * fac[i]
            if s == REACH:
                dqt[:, lo:lo + CH] = part
            else:
                dqt[:, lo:lo + CH] = dqt[:, lo:lo + CH] + part
        term[s, 0] = nt(ds[b], qs[b]).astype(BF)
        give(s, 0)

    mine = pl.ds(pl.multiple_of(xl * QUART, QUART), QUART)
    other = pl.ds(pl.multiple_of((1 - xl) * QUART, QUART), QUART)
    other_rows = pl.ds(pl.multiple_of(core * 256 + (1 - xl) * QUART, QUART), QUART)

    def fold_c(s):
        for j in (1, 0):
            bc[s, j].wait_recv()
            xsend[s, j] = (term[s, j, other_rows].astype(F32) + cbuf[s, j, other].astype(F32)).astype(BF)
            bx[s, j] = send(xsend.at[s, j], xbuf.at[s, j], x_peer)
            hold[s, j] = term[s, j, my_rows].astype(F32) + cbuf[s, j, mine].astype(F32)

    outs = (dk_ref, dv_ref)

    def fold_x(s):
        for j in (1, 0):
            if s in STRAIGHT:
                for cp in bx[s, j]:
                    cp.wait_recv()
            else:
                bx[s, j].wait_recv()
            for k in range(NSUB):
                rows = slice(k * SUB, (k + 1) * SUB)
                if s in STRAIGHT:
                    near = dbuf.at[s - STRAIGHT[0], j]
                    total = term[s, j, sub_rows[k]].astype(F32) + near[0, rows].astype(F32)
                    total = total + near[1, rows].astype(F32) + near[2, rows].astype(F32)
                else:
                    total = hold[s, j, rows] + xbuf[s, j, rows].astype(F32)
                if s < REACH:
                    bz[s + 1, j, k].wait_recv()
                    total = total + zbuf[s, j, rows].astype(F32)
                if s > 0:
                    zsend[s, j, rows] = total.astype(BF)
                    bz[s, j, k] = send(zsend.at[s, j, rows], zbuf.at[s - 1, j, rows], z_prev)
                else:
                    outs[j][sub_rows[k], col] = total.astype(BF)
            if s == 0:
                spread(j)

    ax, aup, adn, xup, xdn = {}, {}, {}, {}, {}

    def spread(j):
        piece = outs[j].at[my_rows, col]
        ax[j] = send(piece, piece, x_peer)
        aup[j] = send(piece, piece, y_next)
        adn[j] = send(piece, piece, y_prev)

    backward(4)
    backward(3)
    backward(2)
    fold_x(4)
    backward(1)
    fold_c(2)
    backward(0)
    fold_x(3)
    fold_c(1)
    fold_c(0)
    for h in range(2):
        o_ref[:, h * HD:(h + 1) * HD] = ot[:, h * BLK:(h + 1) * BLK].T
    fold_x(2)
    for h in range(2):
        dq_ref[:, h * HD:(h + 1) * HD] = (dqt[:, h * BLK:(h + 1) * BLK] * SCALE).astype(BF).T
    fold_x(1)
    fold_x(0)

    below = pl.ds(pl.multiple_of(((y + 3) % 4) * HD, HD), HD)
    above = pl.ds(pl.multiple_of(((y + 1) % 4) * HD, HD), HD)
    across = pl.ds(pl.multiple_of(((y + 2) % 4) * HD, HD), HD)

    def hrow(which, k):
        return pl.ds(pl.multiple_of(core * 256 + which * QUART + k * 64, 64), 64)

    fin = []

    def relay(j, which):
        up = outs[j].at[hrow(which, 0), below]
        dn = outs[j].at[hrow(which, 1), above]
        fin.append(send(up, up, y_next))
        fin.append(send(dn, dn, y_prev))
        fin.append(send(up, up, y_next_o))
        fin.append(send(dn, dn, y_prev_o))

    for j in (1, 0):
        ax[j].wait_recv()
        piece = outs[j].at[other_rows, col]
        xup[j] = send(piece, piece, y_next)
        xdn[j] = send(piece, piece, y_prev)
        piece = outs[j].at[half_rows, col]
        fin.append(send(piece, piece, c_peer))
    for j in (1, 0):
        aup[j].wait_recv()
        adn[j].wait_recv()
        relay(j, xl)
    for j in (1, 0):
        xup[j].wait_recv()
        xdn[j].wait_recv()
        relay(j, 1 - xl)
        for cols in (below, above):
            piece = outs[j].at[half_rows, cols]
            fin.append(send(piece, piece, c_peer))
    for cp in fin:
        cp.wait_recv()
    for cp in sent:
        cp.wait_send()
    assert len(sent) == N_SEND, len(sent)


def place_outputs(*refs):
    n = (len(refs) - 1) // 2
    sem = refs[-1]
    copies = [pltpu.make_async_copy(refs[i], refs[n + i], sem.at[i]) for i in range(n)]
    for cp in copies:
        cp.start()
    for cp in copies:
        cp.wait()


N_SEND = 106


def solution(mesh):
    n_ctx = mesh.shape["ctx"]

    def per_device(queries, keys, values, out_grad, doc_lengths):
        steps = REACH + 1
        vm = pl.BlockSpec(memory_space=pltpu.VMEM)
        hbm = pl.BlockSpec(memory_space=pl.ANY)
        shapes = tuple(jax.ShapeDtypeStruct(a.shape, BF) for a in (queries, queries, keys, values))
        raw = pl.pallas_call(
            functools.partial(kernel, n_ctx, doc_lengths.shape[0]),
            out_shape=shapes,
            in_specs=[hbm, hbm, hbm, hbm, pl.BlockSpec(memory_space=pltpu.SMEM)],
            out_specs=(vm, vm, vm, vm),
            scratch_shapes=[
                pltpu.VMEM((BLK, 256), BF),
                pltpu.VMEM((BLK, 256), BF),
                pltpu.VMEM((steps, 2, BLK, HD), BF),
                pltpu.VMEM((HD, QN), BF),
                pltpu.VMEM((HD, QN), BF),
                pltpu.VMEM((steps, 1, HD, BLK), BF),
                pltpu.VMEM((steps, BLK, QN), BF),
                pltpu.VMEM((steps, BLK, QN), F32),
                pltpu.VMEM((HD, QN), F32),
                pltpu.VMEM((HD, QN), BF),
                pltpu.VMEM((HD, QN), F32),
                pltpu.VMEM((2, HD, QN), BF),
                pltpu.VMEM((2, HD, QN), BF),
                pltpu.VMEM((2, BLK, QN), BF),
                pltpu.VMEM((steps, 2, BLK, HD), BF),
                pltpu.VMEM((steps, 2, 256, HD), BF),
                pltpu.VMEM((len(STRAIGHT), 2, 3, QUART, HD), BF),
                pltpu.VMEM((steps, 2, QUART, HD), F32),
                pltpu.VMEM((steps, 2, QUART, HD), BF),
                pltpu.VMEM((steps, 2, QUART, HD), BF),
                pltpu.VMEM((REACH, 2, QUART, HD), BF),
                pltpu.VMEM((steps, 2, QUART, HD), BF),
                pltpu.SemaphoreType.DMA((4,)),
                pltpu.SemaphoreType.DMA((N_SEND,)),
                pltpu.SemaphoreType.DMA((N_SEND,)),
            ],
            compiler_params=pltpu.CompilerParams(
                collective_id=0, has_side_effects=True, vmem_limit_bytes=40 * 1024 * 1024
            ),
        )(queries, keys, values, out_grad, doc_lengths)
        return pl.pallas_call(
            place_outputs,
            out_shape=shapes,
            in_specs=[vm] * 4,
            out_specs=(hbm,) * 4,
            scratch_shapes=[pltpu.SemaphoreType.DMA((4,))],
        )(*raw)

    return jax.shard_map(
        per_device,
        mesh=mesh,
        in_specs=(P("ctx", "tp"), P("ctx", None), P("ctx", None), P("ctx", "tp"), P()),
        out_specs=(P("ctx", "tp"), P("ctx", "tp"), P("ctx", None), P("ctx", None)),
        check_vma=False,
    )
```

time: 224 us -> 74 us (0.33)
  the two profiles are of different devices: /device:TPU:4 before, /device:TPU:1 now
where the time goes in v1:
time: 74 us; the launch traced here: 73.7 us
  Pallas kernels  65.4 us (88%)
  local copies, waits for them, and re-layouts  7.6 us (10%)
    pallas_call x1, Pallas kernels, per_device(): pl.pallas_call(functools.partial(kernel, n_ctx, doc_lengths.shape[0]), ou...  62.9 us
    unnamed x18, local copies, waits for them, and re-layouts  7.6 us
    pallas_call x1, Pallas kernels, per_device(): pl.pallas_call(place_outputs, out_shape=shapes, in_specs=[vm] * 4, out_sp...  2.53 us

profile of v1, /device:TPU:1, one launch (start us, length us, event | category | flops | bytes accessed | tf_op | source)
XLA Modules:
  0.0 73.7 jit_solution(16919032974229290524)
XLA Ops:
  0.6 0.0 copy-start.2
  0.6 1.0 %copy-done.2 = bf16[512,512]{1,0:T(8,128)(2,1)S(1)} copy-done((bf16[512,512]{1,0:T(8,128)(2,1)S(1)}, bf16[512,512]{1,0:T(8,128)(2,1)}, u32[]{:S(2)}) %copy-start.2) | copy-done | bytes 524312
  1.7 0.0 copy-start.3
  1.7 1.0 %copy-done.3 = bf16[512,512]{1,0:T(8,128)(2,1)S(1)} copy-done((bf16[512,512]{1,0:T(8,128)(2,1)S(1)}, bf16[512,512]{1,0:T(8,128)(2,1)}, u32[]{:S(2)}) %copy-start.3) | copy-done | bytes 524312
  2.7 0.0 copy-start.4
  2.7 0.9 %copy-done.4 = bf16[512,256]{1,0:T(8,128)(2,1)S(1)} copy-done((bf16[512,256]{1,0:T(8,128)(2,1)S(1)}, bf16[512,256]{1,0:T(8,128)(2,1)}, u32[]{:S(2)}) %copy-start.4) | copy-done | bytes 262168
  3.7 0.0 copy-start.5
  3.7 0.9 %copy-done.5 = bf16[512,256]{1,0:T(8,128)(2,1)S(1)} copy-done((bf16[512,256]{1,0:T(8,128)(2,1)S(1)}, bf16[512,256]{1,0:T(8,128)(2,1)}, u32[]{:S(2)}) %copy-start.5) | copy-done | bytes 262168
  4.6 0.0 copy-start.8
  4.6 0.7 copy-done.8
  5.3 62.9 %shard_map.84 = (bf16[512,256]{1,0:T(8,128)(2,1)S(1)}, bf16[512,256]{1,0:T(8,128)(2,1)S(1)}, bf16[512,512]{1,0:T(8,128)(2,1)S(1)}, bf16[512,512]{1,0:T(8,128)(2,1)S(1)}) custom-call(bf16[512,256]{1,0:T(8,128)(2,1)S(1)} %copy-done.4, bf16[512,512]{1,0:T(8,128)(2,1)S(1)} %copy-done.2, bf16[512,512]{1,0:T(8,128)(2,1)S(1)} %copy-done.3, ...), custom_call_target="tpu_custom_call" | custom-call | tf_op jit(solution)/shard_map/pallas_call | solution.py:358
  68.1 0.0 copy-start
  68.1 0.8 %copy-done = bf16[512,512]{1,0:T(8,128)(2,1)} copy-done((bf16[512,512]{1,0:T(8,128)(2,1)}, bf16[512,512]{1,0:T(8,128)(2,1)S(1)}, u32[]{:S(2)}) %copy-start) | copy-done | bytes 524312
  68.9 0.0 copy-start.1
  68.9 0.8 %copy-done.1 = bf16[512,512]{1,0:T(8,128)(2,1)} copy-done((bf16[512,512]{1,0:T(8,128)(2,1)}, bf16[512,512]{1,0:T(8,128)(2,1)S(1)}, u32[]{:S(2)}) %copy-start.1) | copy-done | bytes 524312
  69.7 0.0 copy-start.6
  69.7 0.7 copy-done.6
  70.4 0.0 copy-start.7
  70.4 0.7 copy-done.7
  71.1 2.5 %shard_map.85 = (bf16[512,256]{1,0:T(8,128)(2,1)}, bf16[512,256]{1,0:T(8,128)(2,1)}, bf16[512,512]{1,0:T(8,128)(2,1)}, bf16[512,512]{1,0:T(8,128)(2,1)}) custom-call(bf16[512,256]{1,0:T(8,128)(2,1)} %copy-done.6, bf16[512,256]{1,0:T(8,128)(2,1)} %copy-done.7, bf16[512,512]{1,0:T(8,128)(2,1)} %copy-done, bf16[512,512]{1,0:T(8,128)(2,1)} %copy-done.1), custom_call_target="tpu_custom_call" | custom-call | tf_op jit(solution)/shard_map/pallas_call | solution.py:394
Async XLA Ops:
  0.6 1.0 %copy-start.2 = (bf16[512,512]{1,0:T(8,128)(2,1)S(1)}, bf16[512,512]{1,0:T(8,128)(2,1)}, u32[]{:S(2)}) copy-start(bf16[512,512]{1,0:T(8,128)(2,1)} %k_hbm.1) | copy-start | bytes 1572868
  1.7 1.0 %copy-start.3 = (bf16[512,512]{1,0:T(8,128)(2,1)S(1)}, bf16[512,512]{1,0:T(8,128)(2,1)}, u32[]{:S(2)}) copy-start(bf16[512,512]{1,0:T(8,128)(2,1)} %v_hbm.1) | copy-start | bytes 1572868
  2.7 0.9 %copy-start.4 = (bf16[512,256]{1,0:T(8,128)(2,1)S(1)}, bf16[512,256]{1,0:T(8,128)(2,1)}, u32[]{:S(2)}) copy-start(bf16[512,256]{1,0:T(8,128)(2,1)} %q_hbm.1) | copy-start | bytes 786436
  3.7 0.9 %copy-start.5 = (bf16[512,256]{1,0:T(8,128)(2,1)S(1)}, bf16[512,256]{1,0:T(8,128)(2,1)}, u32[]{:S(2)}) copy-start(bf16[512,256]{1,0:T(8,128)(2,1)} %g_hbm.1) | copy-start | bytes 786436
  4.6 0.7 copy-start.8
  68.1 0.8 %copy-start = (bf16[512,512]{1,0:T(8,128)(2,1)}, bf16[512,512]{1,0:T(8,128)(2,1)S(1)}, u32[]{:S(2)}) copy-start(bf16[512,512]{1,0:T(8,128)(2,1)S(1)} %get-tuple-element.10.refs_2_) | copy-start | bytes 1572868
  68.9 0.8 %copy-start.1 = (bf16[512,512]{1,0:T(8,128)(2,1)}, bf16[512,512]{1,0:T(8,128)(2,1)S(1)}, u32[]{:S(2)}) copy-start(bf16[512,512]{1,0:T(8,128)(2,1)S(1)} %get-tuple-element.11.refs_3_) | copy-start | bytes 1572868
  69.7 0.7 copy-start.6
  70.4 0.7 copy-start.7

commit v2 on v1

--- a/solution.py
+++ b/solution.py
@@ -35,8 +35,8 @@
     return jnp.dot(a, b, preferred_element_type=F32)
 
 
-def kernel(n_ctx, ndoc, q_hbm, k_hbm, v_hbm, g_hbm, len_ref, o_ref, dq_ref, dk_ref, dv_ref,
-           q_in, g_in, kv, qt, gt, kvt, probs, dprob, acc, ot, dqt, gs, qs, ds,
+def kernel(n_ctx, ndoc, q_hbm, k_hbm, v_hbm, g_hbm, len_ref, o_ref, dq_ref, kvg_ref,
+           q_in, g_in, kv, qt, gt, kvt, vtr, probs, dprob, acc, ot, dqt, gs, qs, ds,
            term, cbuf, dbuf, hold, xsend, xbuf, zbuf, zsend, lsem, ssem, rsem):
     c = lax.axis_index("ctx")
     t = lax.axis_index("tp")
@@ -117,18 +117,30 @@
     l_run = [jnp.zeros((1, CH), F32)] * nch
     m_at = {}
 
+    def live_rows(s, off):
+        if s == 0 and off + CH <= BLK // 2:
+            return slice(0, BLK // 2)
+        if s == REACH and off >= BLK // 2:
+            return slice(BLK // 2, BLK)
+        return slice(0, BLK)
+
+    def blank(ref, rows, lo):
+        if rows.stop - rows.start < BLK:
+            skipped = slice(BLK // 2, BLK) if rows.start == 0 else slice(0, BLK // 2)
+            ref[skipped, lo:lo + CH] = jnp.zeros((BLK // 2, CH), BF)
+
     def forward(s):
-        keys, vals = kv[s, 0], kv[s, 1]
-        kvt[s, 0] = keys.T
-        vt = vals.T
+        kvt[s, 0] = kv[s, 0].T
+        vtr[s % 2] = kv[s, 1].T
         for i in range(nch):
             lo = i * CH
             off = (i * CH) % BLK
-            sc = nn(keys, qt[:, lo:lo + CH])
+            rows = live_rows(s, off)
+            sc = nn(kv[s, 0, rows], qt[:, lo:lo + CH])
             first = start[:, off:off + CH] - (c - s) * BLK
-            seen = krow >= first
+            seen = krow[rows] >= first
             if s == 0:
-                seen = seen & (krow <= lane[:, off:off + CH])
+                seen = seen & (krow[rows] <= lane[:, off:off + CH])
             sc = jnp.where(seen, sc, NEG)
             top = jnp.maximum(m_run[i], jnp.max(sc, axis=0, keepdims=True))
             p = jnp.exp2(sc * EXPC - top * EXPC)
@@ -137,13 +149,14 @@
             m_run[i] = top
             m_at[s, i] = top
             pb = p.astype(BF)
-            probs[s, :, lo:lo + CH] = pb
-            part = nn(vt, pb)
+            probs[s, rows, lo:lo + CH] = pb
+            blank(probs.at[s], rows, lo)
+            part = nn(vtr[s % 2, :, rows], pb)
             if s == 0:
                 acc[:, lo:lo + CH] = part
             else:
                 acc[:, lo:lo + CH] = acc[:, lo:lo + CH] * fade + part
-            dprob[s, :, lo:lo + CH] = nn(vals, gt[:, lo:lo + CH])
+            dprob[s, rows, lo:lo + CH] = nn(kv[s, 1, rows], gt[:, lo:lo + CH])
 
     def take_z(s):
         for j in range(2):
@@ -217,9 +230,11 @@
             finish()
         for i in range(nch):
             lo = i * CH
-            dsc = (probs[s, :, lo:lo + CH].astype(F32) * (dprob[s, :, lo:lo + CH] - delta[i])).astype(BF)
-            ds[b, :, lo:lo + CH] = dsc
-            part = nn(kvt[s, 0], dsc) * fac[i]
+            rows = live_rows(s, lo % BLK)
+            dsc = (probs[s, rows, lo:lo + CH].astype(F32) * (dprob[s, rows, lo:lo + CH] - delta[i])).astype(BF)
+            ds[b, rows, lo:lo + CH] = dsc
+            blank(ds.at[b], rows, lo)
+            part = nn(kvt[s, 0, :, rows], dsc) * fac[i]
             if s == REACH:
                 dqt[:, lo:lo + CH] = part
             else:
@@ -238,7 +253,6 @@
             bx[s, j] = send(xsend.at[s, j], xbuf.at[s, j], x_peer)
             hold[s, j] = term[s, j, my_rows].astype(F32) + cbuf[s, j, mine].astype(F32)
 
-    outs = (dk_ref, dv_ref)
 
     def fold_x(s):
         for j in (1, 0):
@@ -262,14 +276,14 @@
                     zsend[s, j, rows] = total.astype(BF)
                     bz[s, j, k] = send(zsend.at[s, j, rows], zbuf.at[s - 1, j, rows], z_prev)
                 else:
-                    outs[j][sub_rows[k], col] = total.astype(BF)
+                    kvg_ref[j, y, sub_rows[k]] = total.astype(BF)
             if s == 0:
                 spread(j)
 
     ax, aup, adn, xup, xdn = {}, {}, {}, {}, {}
 
     def spread(j):
-        piece = outs[j].at[my_rows, col]
+        piece = kvg_ref.at[j, y, my_rows]
         ax[j] = send(piece, piece, x_peer)
         aup[j] = send(piece, piece, y_next)
         adn[j] = send(piece, piece, y_prev)
@@ -292,9 +306,8 @@
     fold_x(1)
     fold_x(0)
 
-    below = pl.ds(pl.multiple_of(((y + 3) % 4) * HD, HD), HD)
-    above = pl.ds(pl.multiple_of(((y + 1) % 4) * HD, HD), HD)
-    across = pl.ds(pl.multiple_of(((y + 2) % 4) * HD, HD), HD)
+    below = (y + 3) % 4
+    above = (y + 1) % 4
 
     def hrow(which, k):
         return pl.ds(pl.multiple_of(core * 256 + which * QUART + k * 64, 64), 64)
@@ -302,8 +315,8 @@
     fin = []
 
     def relay(j, which):
-        up = outs[j].at[hrow(which, 0), below]
-        dn = outs[j].at[hrow(which, 1), above]
+        up = kvg_ref.at[j, below, hrow(which, 0)]
+        dn = kvg_ref.at[j, above, hrow(which, 1)]
         fin.append(send(up, up, y_next))
         fin.append(send(dn, dn, y_prev))
         fin.append(send(up, up, y_next_o))
@@ -311,10 +324,10 @@
 
     for j in (1, 0):
         ax[j].wait_recv()
-        piece = outs[j].at[other_rows, col]
+        piece = kvg_ref.at[j, y, other_rows]
         xup[j] = send(piece, piece, y_next)
         xdn[j] = send(piece, piece, y_prev)
-        piece = outs[j].at[half_rows, col]
+        piece = kvg_ref.at[j, y, half_rows]
         fin.append(send(piece, piece, c_peer))
     for j in (1, 0):
         aup[j].wait_recv()
@@ -325,7 +338,7 @@
         xdn[j].wait_recv()
         relay(j, 1 - xl)
         for cols in (below, above):
-            piece = outs[j].at[half_rows, cols]
+            piece = kvg_ref.at[j, cols, half_rows]
             fin.append(send(piece, piece, c_peer))
     for cp in fin:
         cp.wait_recv()
@@ -334,13 +347,20 @@
     assert len(sent) == N_SEND, len(sent)
 
 
-def place_outputs(*refs):
-    n = (len(refs) - 1) // 2
-    sem = refs[-1]
-    copies = [pltpu.make_async_copy(refs[i], refs[n + i], sem.at[i]) for i in range(n)]
-    for cp in copies:
+def place_outputs(o_raw, dq_raw, kvg_raw, o_out, dq_out, dk_out, dv_out, o_v, dq_v, kvg_v, isem, osem):
+    fetch = [pltpu.make_async_copy(o_raw, o_v, isem.at[0]), pltpu.make_async_copy(dq_raw, dq_v, isem.at[1])]
+    store = [pltpu.make_async_copy(o_v, o_out, osem.at[0]), pltpu.make_async_copy(dq_v, dq_out, osem.at[1])]
+    for j, out in enumerate((dk_out, dv_out)):
+        for g in range(KVH):
+            i = len(fetch)
+            fetch.append(pltpu.make_async_copy(kvg_raw.at[j, g], kvg_v.at[j, g], isem.at[i]))
+            store.append(pltpu.make_async_copy(kvg_v.at[j, g], out.at[:, g * HD:(g + 1) * HD], osem.at[i]))
+    for cp in fetch:
         cp.start()
-    for cp in copies:
+    for get, put in zip(fetch, store):
+        get.wait()
+        put.start()
+    for cp in store:
         cp.wait()
 
 
@@ -357,9 +377,9 @@
         shapes = tuple(jax.ShapeDtypeStruct(a.shape, BF) for a in (queries, queries, keys, values))
         raw = pl.pallas_call(
             functools.partial(kernel, n_ctx, doc_lengths.shape[0]),
-            out_shape=shapes,
+            out_shape=shapes[:2] + (jax.ShapeDtypeStruct((2, KVH, BLK, HD), BF),),
             in_specs=[hbm, hbm, hbm, hbm, pl.BlockSpec(memory_space=pltpu.SMEM)],
-            out_specs=(vm, vm, vm, vm),
+            out_specs=(vm, vm, vm),
             scratch_shapes=[
                 pltpu.VMEM((BLK, 256), BF),
                 pltpu.VMEM((BLK, 256), BF),
@@ -367,6 +387,7 @@
                 pltpu.VMEM((HD, QN), BF),
                 pltpu.VMEM((HD, QN), BF),
                 pltpu.VMEM((steps, 1, HD, BLK), BF),
+                pltpu.VMEM((2, HD, BLK), BF),
                 pltpu.VMEM((steps, BLK, QN), BF),
                 pltpu.VMEM((steps, BLK, QN), F32),
                 pltpu.VMEM((HD, QN), F32),
@@ -388,15 +409,22 @@
                 pltpu.SemaphoreType.DMA((N_SEND,)),
             ],
             compiler_params=pltpu.CompilerParams(
-                collective_id=0, has_side_effects=True, vmem_limit_bytes=40 * 1024 * 1024
+                collective_id=0, has_side_effects=True, vmem_limit_bytes=60 * 1024 * 1024
             ),
         )(queries, keys, values, out_grad, doc_lengths)
         return pl.pallas_call(
             place_outputs,
             out_shape=shapes,
-            in_specs=[vm] * 4,
+            in_specs=[hbm] * 3,
             out_specs=(hbm,) * 4,
-            scratch_shapes=[pltpu.SemaphoreType.DMA((4,))],
+            scratch_shapes=[
+                pltpu.VMEM((BLK, 256), BF),
+                pltpu.VMEM((BLK, 256), BF),
+                pltpu.VMEM((2, KVH, BLK, HD), BF),
+                pltpu.SemaphoreType.DMA((10,)),
+                pltpu.SemaphoreType.DMA((10,)),
+            ],
+            compiler_params=pltpu.CompilerParams(vmem_limit_bytes=62 * 1024 * 1024),
         )(*raw)
 
     return jax.shard_map(

time: 74 us -> 67.4 us (0.911)
  local copies, waits for them, and re-layouts: 7.6 us -> 0 us
  Pallas kernels: 65.4 us -> 66.6 us
    unnamed x18 -> x0, local copies, waits for them, and re-layouts: 7.6 us -> none
    pallas_call x1, Pallas kernels: 62.9 us -> 64.3 us  [per_device(): pl.pallas_call(functools.partial(kernel, n_ctx, doc_lengths.shape[0]), ou...]
where the time goes in v2:
time: 67.4 us; the launch traced here: 67.2 us
  Pallas kernels  66.6 us (99%)
    pallas_call x1, Pallas kernels, per_device(): pl.pallas_call(functools.partial(kernel, n_ctx, doc_lengths.shape[0]), ou...  64.3 us
    pallas_call x1, Pallas kernels, per_device(): pl.pallas_call(place_outputs, out_shape=shapes, in_specs=[hbm] * 3, out_s...  2.25 us

profile of v2, /device:TPU:1, one launch (start us, length us, event | category | flops | bytes accessed | tf_op | source)
XLA Modules:
  0.0 67.2 jit_solution(3909180410408137962)
XLA Ops:
  0.6 64.3 %shard_map.84 = (bf16[512,256]{1,0:T(8,128)(2,1)}, bf16[512,256]{1,0:T(8,128)(2,1)}, bf16[2,4,512,128]{3,2,1,0:T(8,128)(2,1)}) custom-call(bf16[512,256]{1,0:T(8,128)(2,1)} %q_hbm.1, bf16[512,512]{1,0:T(8,128)(2,1)} %k_hbm.1, bf16[512,512]{1,0:T(8,128)(2,1)} %v_hbm.1, bf16[512,256]{1,0:T(8,128)(2,1)} %g_hbm.1, s32[32]{0:T(128)} %len_ref.1), custom_call_target="tpu_custom_call" | custom-call | tf_op jit(solution)/shard_map/pallas_call | solution.py:378
  65.0 2.3 %shard_map.85 = (bf16[512,256]{1,0:T(8,128)(2,1)}, bf16[512,256]{1,0:T(8,128)(2,1)}, bf16[512,512]{1,0:T(8,128)(2,1)}, bf16[512,512]{1,0:T(8,128)(2,1)}) custom-call(bf16[512,256]{1,0:T(8,128)(2,1)} %get-tuple-element.7.o_raw, bf16[512,256]{1,0:T(8,128)(2,1)} %get-tuple-element.8.dq_raw, bf16[2,4,512,128]{3,2,1,0:T(8,128)(2,1)} %get-tuple-element.9.kvg_raw), custom_call_target="tpu_custom_call" | custom-call | tf_op jit(solution)/shard_map/pallas_call | solution.py:415

commit v3 on v2

--- a/solution.py
+++ b/solution.py
@@ -15,6 +15,7 @@
 BLK = 512
 QN = 1024
 CH = 256
+RB = 128
 QUART = 128
 NSUB = 2
 SUB = QUART // NSUB
@@ -36,7 +37,7 @@
 
 
 def kernel(n_ctx, ndoc, q_hbm, k_hbm, v_hbm, g_hbm, len_ref, o_ref, dq_ref, kvg_ref,
-           q_in, g_in, kv, qt, gt, kvt, vtr, probs, dprob, acc, ot, dqt, gs, qs, ds,
+           q_in, g_in, kv, qt, gt, kvt, vtr, kx, sbuf, probs, dprob, acc, ot, dqt, gs, qs, ds,
            term, cbuf, dbuf, hold, xsend, xbuf, zbuf, zsend, lsem, ssem, rsem):
     c = lax.axis_index("ctx")
     t = lax.axis_index("tp")
@@ -77,44 +78,64 @@
         cp.start()
 
     barrier = pltpu.get_barrier_semaphore()
-    peers = (z_next, z_prev, x_peer, c_peer, y_next, y_prev, x_diag, y_next_o, y_prev_o)
+    peers = (x_peer, c_peer, y_next, y_prev, x_diag, y_next_o, y_prev_o)
+    for dev, ok in ((z_next, c < n_ctx - 1), (z_prev, c > 0)):
+        @pl.when(ok)
+        def _(dev=dev):
+            pl.semaphore_signal(barrier, inc=1, device_id=dev, device_id_type=MESH)
+
     for dev in peers:
         pl.semaphore_signal(barrier, inc=1, device_id=dev, device_id_type=MESH)
-    pl.semaphore_wait(barrier, len(peers))
+    pl.semaphore_wait(barrier, len(peers) + jnp.minimum(c, 1) + jnp.minimum(n_ctx - 1 - c, 1))
 
     sent = []
 
-    def send(src, dst, dev):
+    def only(ok, act):
+        if ok is None:
+            act()
+        else:
+            pl.when(ok)(act)
+
+    def send(src, dst, dev, ok=None):
         i = len(sent)
         cp = pltpu.make_async_remote_copy(src_ref=src, dst_ref=dst, send_sem=ssem.at[i], recv_sem=rsem.at[i],
                                           device_id=dev, device_id_type=MESH)
-        cp.start()
-        sent.append(cp)
+        only(ok, lambda: cp.start())
+        sent.append((cp, ok))
         return cp
 
     zc, xc, cc, dc = {}, {}, {}, {}
     for j, src in ((0, k_hbm), (1, v_hbm)):
         for k in range(NSUB):
-            zc[1, j, k] = send(src.at[sub_rows[k], col], kv.at[1, j, sub_rows[k]], z_next)
+            zc[1, j, k] = send(src.at[sub_rows[k], col], kv.at[1, j, sub_rows[k]], z_next, c < n_ctx - 1)
 
     lane = lax.broadcasted_iota(jnp.int32, (1, BLK), 1)
-    pos = lane + c * BLK
-    start = jnp.zeros((1, BLK), jnp.int32)
+    dlane = lax.broadcasted_iota(jnp.int32, (1, HD), 1)
+    drow = lax.broadcasted_iota(jnp.int32, (HD, 1), 0)
+    lo_l, hi_l = jnp.zeros((1, HD), jnp.int32), jnp.zeros((1, HD), jnp.int32)
+    lo_r, hi_r = jnp.zeros((HD, 1), jnp.int32), jnp.zeros((HD, 1), jnp.int32)
     end = jnp.int32(0)
     for d in range(ndoc):
+        lo_l, lo_r = jnp.where(dlane == d, end, lo_l), jnp.where(drow == d, end, lo_r)
         end = end + len_ref[d]
-        start = jnp.where(pos >= end, end, start)
-    krow = lax.broadcasted_iota(jnp.int32, (BLK, CH), 0)
+        hi_l, hi_r = jnp.where(dlane == d, end, hi_l), jnp.where(drow == d, end, hi_r)
+    lo_l = jnp.where(dlane == ndoc, -(1 << 30), lo_l)
+    pos = lane + c * BLK
+    block_doc = jnp.where((pos >= lo_r) & (pos < hi_r), 0.0, NEG).astype(BF)
+    kpos0 = lax.broadcasted_iota(jnp.int32, (BLK, HD), 0) + c * BLK
+    krow = lax.broadcasted_iota(jnp.int32, (RB, CH), 0)
+    for b in range(2):
+        vtr[b, HD:] = jnp.ones((8, BLK), BF)
 
     for cp in loads:
         cp.wait()
     for h in range(2):
-        qt[:, h * BLK:(h + 1) * BLK] = q_in[:, h * HD:(h + 1) * HD].T
+        qt[:HD, h * BLK:(h + 1) * BLK] = q_in[:, h * HD:(h + 1) * HD].T
+        qt[HD:, h * BLK:(h + 1) * BLK] = block_doc
         gt[:, h * BLK:(h + 1) * BLK] = g_in[:, h * HD:(h + 1) * HD].T
 
     nch = QN // CH
     m_run = [jnp.full((1, CH), FLOOR, F32)] * nch
-    l_run = [jnp.zeros((1, CH), F32)] * nch
     m_at = {}
 
     def live_rows(s, off):
@@ -130,40 +151,54 @@
             ref[skipped, lo:lo + CH] = jnp.zeros((BLK // 2, CH), BF)
 
     def forward(s):
+        b = s % 2
         kvt[s, 0] = kv[s, 0].T
-        vtr[s % 2] = kv[s, 1].T
+        vtr[b, :HD] = kv[s, 1].T
+        kx[b, :, :HD] = kv[s, 0]
+        kpos = kpos0 - s * BLK
+        kx[b, :, HD:] = jnp.where((kpos >= lo_l) & (kpos < hi_l), 1.0, 0.0).astype(BF)
         for i in range(nch):
             lo = i * CH
             off = (i * CH) % BLK
+            cols = slice(lo, lo + CH)
             rows = live_rows(s, off)
-            sc = nn(kv[s, 0, rows], qt[:, lo:lo + CH])
-            first = start[:, off:off + CH] - (c - s) * BLK
-            seen = krow[rows] >= first
-            if s == 0:
-                seen = seen & (krow[rows] <= lane[:, off:off + CH])
-            sc = jnp.where(seen, sc, NEG)
-            top = jnp.maximum(m_run[i], jnp.max(sc, axis=0, keepdims=True))
-            p = jnp.exp2(sc * EXPC - top * EXPC)
+            pieces = [slice(r, r + RB) for r in range(rows.start, rows.stop, RB)]
+            top = m_run[i]
+            for piece in pieces:
+                sc = nn(kx[b, piece], qt[:, cols])
+                if s == 0 and piece.stop > off:
+                    sc = jnp.where(krow + piece.start <= lane[:, off:off + CH], sc, NEG)
+                sbuf[i % 2, piece] = sc
+                top = jnp.maximum(top, jnp.max(sc, axis=0, keepdims=True))
+            scaled = top * EXPC
+            for piece in pieces:
+                probs[s, piece, cols] = jnp.exp2(sbuf[i % 2, piece] * EXPC - scaled).astype(BF)
             fade = jnp.exp2((m_run[i] - top) * EXPC)
-            l_run[i] = l_run[i] * fade + jnp.sum(p, axis=0, keepdims=True)
             m_run[i] = top
             m_at[s, i] = top
-            pb = p.astype(BF)
-            probs[s, rows, lo:lo + CH] = pb
             blank(probs.at[s], rows, lo)
-            part = nn(vtr[s % 2, :, rows], pb)
+            part = nn(vtr[b, :, rows], probs[s, rows, cols])
             if s == 0:
-                acc[:, lo:lo + CH] = part
+                acc[:, cols] = part
             else:
-                acc[:, lo:lo + CH] = acc[:, lo:lo + CH] * fade + part
-            dprob[s, rows, lo:lo + CH] = nn(kv[s, 1, rows], gt[:, lo:lo + CH])
+                acc[:, cols] = acc[:, cols] * fade + part
+            for piece in pieces:
+                dprob[s, piece, cols] = nn(kv[s, 1, piece], gt[:, cols])
 
     def take_z(s):
         for j in range(2):
             for k in range(NSUB):
-                zc[s, j, k].wait_recv()
+                @pl.when(c >= s)
+                def _():
+                    zc[s, j, k].wait_recv()
+
+                @pl.when(c < s)
+                def _():
+                    kv[s, j, sub_rows[k]] = jnp.zeros((SUB, HD), BF)
+
                 if s < REACH:
-                    zc[s + 1, j, k] = send(kv.at[s, j, sub_rows[k]], kv.at[s + 1, j, sub_rows[k]], z_next)
+                    zc[s + 1, j, k] = send(kv.at[s, j, sub_rows[k]], kv.at[s + 1, j, sub_rows[k]], z_next,
+                                           (c >= s) & (c < n_ctx - 1))
             piece = kv.at[s, j, my_rows]
             xc[s, j] = send(piece, piece, x_peer)
             if s == REACH:
@@ -196,12 +231,12 @@
 
     inv, delta = [], []
     for i in range(nch):
-        inv.append(1.0 / l_run[i])
+        inv.append(1.0 / acc[HD:HD + 1, i * CH:(i + 1) * CH])
 
     def finish():
         for i in range(nch):
             lo = i * CH
-            out = (acc[:, lo:lo + CH] * inv[i]).astype(BF)
+            out = (acc[:HD, lo:lo + CH] * inv[i]).astype(BF)
             ot[:, lo:lo + CH] = out
             delta.append(jnp.sum(gt[:, lo:lo + CH].astype(F32) * out.astype(F32), axis=0, keepdims=True))
 
@@ -223,7 +258,7 @@
         for i in range(nch):
             lo = i * CH
             gs[b, :, lo:lo + CH] = (gt[:, lo:lo + CH].astype(F32) * fac[i]).astype(BF)
-            qs[b, :, lo:lo + CH] = (qt[:, lo:lo + CH].astype(F32) * (fac[i] * SCALE)).astype(BF)
+            qs[b, :, lo:lo + CH] = (qt[:HD, lo:lo + CH].astype(F32) * (fac[i] * SCALE)).astype(BF)
         term[s, 1] = nt(probs[s], gs[b]).astype(BF)
         give(s, 1)
         if s == REACH:
@@ -231,10 +266,12 @@
         for i in range(nch):
             lo = i * CH
             rows = live_rows(s, lo % BLK)
-            dsc = (probs[s, rows, lo:lo + CH].astype(F32) * (dprob[s, rows, lo:lo + CH] - delta[i])).astype(BF)
-            ds[b, rows, lo:lo + CH] = dsc
+            cols = slice(lo, lo + CH)
+            for r in range(rows.start, rows.stop, RB):
+                piece = slice(r, r + RB)
+                ds[b, piece, cols] = (probs[s, piece, cols].astype(F32) * (dprob[s, piece, cols] - delta[i])).astype(BF)
             blank(ds.at[b], rows, lo)
-            part = nn(kvt[s, 0, :, rows], dsc) * fac[i]
+            part = nn(kvt[s, 0, :, rows], ds[b, rows, cols]) * fac[i]
             if s == REACH:
                 dqt[:, lo:lo + CH] = part
             else:
@@ -270,11 +307,18 @@
                 else:
                     total = hold[s, j, rows] + xbuf[s, j, rows].astype(F32)
                 if s < REACH:
-                    bz[s + 1, j, k].wait_recv()
+                    @pl.when((c >= s) & (c < n_ctx - 1))
+                    def _():
+                        bz[s + 1, j, k].wait_recv()
+
+                    @pl.when((c < s) | (c == n_ctx - 1))
+                    def _():
+                        zbuf[s, j, rows] = jnp.zeros((SUB, HD), BF)
+
                     total = total + zbuf[s, j, rows].astype(F32)
                 if s > 0:
                     zsend[s, j, rows] = total.astype(BF)
-                    bz[s, j, k] = send(zsend.at[s, j, rows], zbuf.at[s - 1, j, rows], z_prev)
+                    bz[s, j, k] = send(zsend.at[s, j, rows], zbuf.at[s - 1, j, rows], z_prev, c >= s)
                 else:
                     kvg_ref[j, y, sub_rows[k]] = total.astype(BF)
             if s == 0:
@@ -342,8 +386,8 @@
             fin.append(send(piece, piece, c_peer))
     for cp in fin:
         cp.wait_recv()
-    for cp in sent:
-        cp.wait_send()
+    for cp, ok in sent:
+        only(ok, lambda: cp.wait_send())
     assert len(sent) == N_SEND, len(sent)
 
 
@@ -384,13 +428,15 @@
                 pltpu.VMEM((BLK, 256), BF),
                 pltpu.VMEM((BLK, 256), BF),
                 pltpu.VMEM((steps, 2, BLK, HD), BF),
-                pltpu.VMEM((HD, QN), BF),
+                pltpu.VMEM((2 * HD, QN), BF),
                 pltpu.VMEM((HD, QN), BF),
                 pltpu.VMEM((steps, 1, HD, BLK), BF),
-                pltpu.VMEM((2, HD, BLK), BF),
+                pltpu.VMEM((2, HD + 8, BLK), BF),
+                pltpu.VMEM((2, BLK, 2 * HD), BF),
+                pltpu.VMEM((2, BLK, CH), F32),
                 pltpu.VMEM((steps, BLK, QN), BF),
                 pltpu.VMEM((steps, BLK, QN), F32),
-                pltpu.VMEM((HD, QN), F32),
+                pltpu.VMEM((HD + 8, QN), F32),
                 pltpu.VMEM((HD, QN), BF),
                 pltpu.VMEM((HD, QN), F32),
                 pltpu.VMEM((2, HD, QN), BF),

time: 67.4 us -> 65.1 us (0.966)
  the two profiles are of different devices: /device:TPU:1 before, /device:TPU:7 now
where the time goes in v3:
time: 65.1 us; the launch traced here: 64.8 us
  Pallas kernels  64 us (98%)
  between operations  0.8 us (1%)
    pallas_call x1, Pallas kernels, per_device(): pl.pallas_call(functools.partial(kernel, n_ctx, doc_lengths.shape[0]), ou...  61.7 us
    pallas_call x1, Pallas kernels, per_device(): pl.pallas_call(place_outputs, out_shape=shapes, in_specs=[hbm] * 3, out_s...  2.25 us

profile of v3, /device:TPU:7, one launch (start us, length us, event | category | flops | bytes accessed | tf_op | source)
XLA Modules:
  0.0 64.8 jit_solution(12883284777049539161)
XLA Ops:
  0.6 61.7 %shard_map.84 = (bf16[512,256]{1,0:T(8,128)(2,1)}, bf16[512,256]{1,0:T(8,128)(2,1)}, bf16[2,4,512,128]{3,2,1,0:T(8,128)(2,1)}) custom-call(bf16[512,256]{1,0:T(8,128)(2,1)} %q_hbm.1, bf16[512,512]{1,0:T(8,128)(2,1)} %k_hbm.1, bf16[512,512]{1,0:T(8,128)(2,1)} %v_hbm.1, bf16[512,256]{1,0:T(8,128)(2,1)} %g_hbm.1, s32[32]{0:T(128)} %len_ref.1), custom_call_target="tpu_custom_call" | custom-call | tf_op jit(solution)/shard_map/pallas_call | solution.py:422
  62.4 2.3 %shard_map.85 = (bf16[512,256]{1,0:T(8,128)(2,1)}, bf16[512,256]{1,0:T(8,128)(2,1)}, bf16[512,512]{1,0:T(8,128)(2,1)}, bf16[512,512]{1,0:T(8,128)(2,1)}) custom-call(bf16[512,256]{1,0:T(8,128)(2,1)} %get-tuple-element.7.o_raw, bf16[512,256]{1,0:T(8,128)(2,1)} %get-tuple-element.8.dq_raw, bf16[2,4,512,128]{3,2,1,0:T(8,128)(2,1)} %get-tuple-element.9.kvg_raw), custom_call_target="tpu_custom_call" | custom-call | tf_op jit(solution)/shard_map/pallas_call | solution.py:461

commit v4 on v3

--- a/solution.py
+++ b/solution.py
@@ -38,7 +38,7 @@
 
 def kernel(n_ctx, ndoc, q_hbm, k_hbm, v_hbm, g_hbm, len_ref, o_ref, dq_ref, kvg_ref,
            q_in, g_in, kv, qt, gt, kvt, vtr, kx, sbuf, probs, dprob, acc, ot, dqt, gs, qs, ds,
-           term, cbuf, dbuf, hold, xsend, xbuf, zbuf, zsend, lsem, ssem, rsem):
+           term, cbuf, dbuf, hold, xsend, xbuf, zbuf, zsend, stage, o_v, dq_v, ksem, lsem, ssem, rsem):
     c = lax.axis_index("ctx")
     t = lax.axis_index("tp")
     half_ctx = n_ctx // 2
@@ -86,6 +86,8 @@
 
     for dev in peers:
         pl.semaphore_signal(barrier, inc=1, device_id=dev, device_id_type=MESH)
+    for cp in loads[2:]:
+        cp.wait()
     pl.semaphore_wait(barrier, len(peers) + jnp.minimum(c, 1) + jnp.minimum(n_ctx - 1 - c, 1))
 
     sent = []
@@ -104,10 +106,17 @@
         sent.append((cp, ok))
         return cp
 
+    settled = [0]
+
+    def settle(upto):
+        for cp, ok in sent[settled[0]:upto]:
+            only(ok, lambda: cp.wait_send())
+        settled[0] = upto
+
     zc, xc, cc, dc = {}, {}, {}, {}
-    for j, src in ((0, k_hbm), (1, v_hbm)):
+    for j in range(2):
         for k in range(NSUB):
-            zc[1, j, k] = send(src.at[sub_rows[k], col], kv.at[1, j, sub_rows[k]], z_next, c < n_ctx - 1)
+            zc[1, j, k] = send(kv.at[0, j, sub_rows[k]], kv.at[1, j, sub_rows[k]], z_next, c < n_ctx - 1)
 
     lane = lax.broadcasted_iota(jnp.int32, (1, BLK), 1)
     dlane = lax.broadcasted_iota(jnp.int32, (1, HD), 1)
@@ -127,7 +136,7 @@
     for b in range(2):
         vtr[b, HD:] = jnp.ones((8, BLK), BF)
 
-    for cp in loads:
+    for cp in loads[:2]:
         cp.wait()
     for h in range(2):
         qt[:HD, h * BLK:(h + 1) * BLK] = q_in[:, h * HD:(h + 1) * HD].T
@@ -320,21 +329,30 @@
                     zsend[s, j, rows] = total.astype(BF)
                     bz[s, j, k] = send(zsend.at[s, j, rows], zbuf.at[s - 1, j, rows], z_prev, c >= s)
                 else:
-                    kvg_ref[j, y, sub_rows[k]] = total.astype(BF)
+                    stage[j, y, sub_rows[k]] = total.astype(BF)
             if s == 0:
                 spread(j)
 
     ax, aup, adn, xup, xdn = {}, {}, {}, {}, {}
 
     def spread(j):
-        piece = kvg_ref.at[j, y, my_rows]
+        piece = stage.at[j, y, my_rows]
         ax[j] = send(piece, piece, x_peer)
         aup[j] = send(piece, piece, y_next)
         adn[j] = send(piece, piece, y_prev)
 
+    kept = []
+
+    def keep(src, dst):
+        cp = pltpu.make_async_copy(src, dst, ksem.at[len(kept)])
+        cp.start()
+        kept.append(cp)
+
+    first_part = len(sent)
     backward(4)
     backward(3)
     backward(2)
+    settle(first_part)
     fold_x(4)
     backward(1)
     fold_c(2)
@@ -343,11 +361,15 @@
     fold_c(1)
     fold_c(0)
     for h in range(2):
-        o_ref[:, h * HD:(h + 1) * HD] = ot[:, h * BLK:(h + 1) * BLK].T
+        o_v[:, h * HD:(h + 1) * HD] = ot[:, h * BLK:(h + 1) * BLK].T
+    keep(o_v, o_ref)
     fold_x(2)
     for h in range(2):
-        dq_ref[:, h * HD:(h + 1) * HD] = (dqt[:, h * BLK:(h + 1) * BLK] * SCALE).astype(BF).T
+        dq_v[:, h * HD:(h + 1) * HD] = (dqt[:, h * BLK:(h + 1) * BLK] * SCALE).astype(BF).T
+    keep(dq_v, dq_ref)
+    second_part = len(sent)
     fold_x(1)
+    settle(second_part)
     fold_x(0)
 
     below = (y + 3) % 4
@@ -359,20 +381,26 @@
     fin = []
 
     def relay(j, which):
-        up = kvg_ref.at[j, below, hrow(which, 0)]
-        dn = kvg_ref.at[j, above, hrow(which, 1)]
-        fin.append(send(up, up, y_next))
-        fin.append(send(dn, dn, y_prev))
-        fin.append(send(up, up, y_next_o))
-        fin.append(send(dn, dn, y_prev_o))
+        up = stage.at[j, below, hrow(which, 0)]
+        dn = stage.at[j, above, hrow(which, 1)]
+        up_out = kvg_ref.at[j, below, hrow(which, 0)]
+        dn_out = kvg_ref.at[j, above, hrow(which, 1)]
+        fin.append(send(up, up_out, y_next))
+        fin.append(send(dn, dn_out, y_prev))
+        fin.append(send(up, up_out, y_next_o))
+        fin.append(send(dn, dn_out, y_prev_o))
+
+    def share(j, g):
+        piece, out = stage.at[j, g, half_rows], kvg_ref.at[j, g, half_rows]
+        fin.append(send(piece, out, c_peer))
+        keep(piece, out)
 
     for j in (1, 0):
         ax[j].wait_recv()
-        piece = kvg_ref.at[j, y, other_rows]
+        piece = stage.at[j, y, other_rows]
         xup[j] = send(piece, piece, y_next)
         xdn[j] = send(piece, piece, y_prev)
-        piece = kvg_ref.at[j, y, half_rows]
-        fin.append(send(piece, piece, c_peer))
+        share(j, y)
     for j in (1, 0):
         aup[j].wait_recv()
         adn[j].wait_recv()
@@ -382,12 +410,12 @@
         xdn[j].wait_recv()
         relay(j, 1 - xl)
         for cols in (below, above):
-            piece = kvg_ref.at[j, cols, half_rows]
-            fin.append(send(piece, piece, c_peer))
+            share(j, cols)
     for cp in fin:
         cp.wait_recv()
-    for cp, ok in sent:
-        only(ok, lambda: cp.wait_send())
+    settle(len(sent))
+    for cp in kept:
+        cp.wait()
     assert len(sent) == N_SEND, len(sent)
 
 
@@ -416,14 +444,13 @@
 
     def per_device(queries, keys, values, out_grad, doc_lengths):
         steps = REACH + 1
-        vm = pl.BlockSpec(memory_space=pltpu.VMEM)
         hbm = pl.BlockSpec(memory_space=pl.ANY)
         shapes = tuple(jax.ShapeDtypeStruct(a.shape, BF) for a in (queries, queries, keys, values))
         raw = pl.pallas_call(
             functools.partial(kernel, n_ctx, doc_lengths.shape[0]),
             out_shape=shapes[:2] + (jax.ShapeDtypeStruct((2, KVH, BLK, HD), BF),),
             in_specs=[hbm, hbm, hbm, hbm, pl.BlockSpec(memory_space=pltpu.SMEM)],
-            out_specs=(vm, vm, vm),
+            out_specs=(hbm, hbm, hbm),
             scratch_shapes=[
                 pltpu.VMEM((BLK, 256), BF),
                 pltpu.VMEM((BLK, 256), BF),
@@ -450,6 +477,10 @@
                 pltpu.VMEM((steps, 2, QUART, HD), BF),
                 pltpu.VMEM((REACH, 2, QUART, HD), BF),
                 pltpu.VMEM((steps, 2, QUART, HD), BF),
+                pltpu.VMEM((2, KVH, BLK, HD), BF),
+                pltpu.VMEM((BLK, 256), BF),
+                pltpu.VMEM((BLK, 256), BF),
+                pltpu.SemaphoreType.DMA((8,)),
                 pltpu.SemaphoreType.DMA((4,)),
                 pltpu.SemaphoreType.DMA((N_SEND,)),
                 pltpu.SemaphoreType.DMA((N_SEND,)),

time: 65.1 us -> 63.9 us (0.982)
  Pallas kernels: 64 us -> 62.5 us
    pallas_call x1, Pallas kernels: 61.7 us -> 60.3 us  [per_device(): pl.pallas_call(functools.partial(kernel, n_ctx, doc_lengths.shape[0]), ou...]
where the time goes in v4:
time: 63.9 us; the launch traced here: 63.3 us
  Pallas kernels  62.5 us (98%)
  between operations  0.8 us (1%)
    pallas_call x1, Pallas kernels, per_device(): pl.pallas_call(functools.partial(kernel, n_ctx, doc_lengths.shape[0]), ou...  60.3 us
    pallas_call x1, Pallas kernels, per_device(): pl.pallas_call(place_outputs, out_shape=shapes, in_specs=[hbm] * 3, out_s...  2.25 us

profile of v4, /device:TPU:7, one launch (start us, length us, event | category | flops | bytes accessed | tf_op | source)
XLA Modules:
  0.0 63.3 jit_solution(1274761053225160922)
XLA Ops:
  0.6 60.3 %shard_map.84 = (bf16[512,256]{1,0:T(8,128)(2,1)}, bf16[512,256]{1,0:T(8,128)(2,1)}, bf16[2,4,512,128]{3,2,1,0:T(8,128)(2,1)}) custom-call(bf16[512,256]{1,0:T(8,128)(2,1)} %q_hbm.1, bf16[512,512]{1,0:T(8,128)(2,1)} %k_hbm.1, bf16[512,512]{1,0:T(8,128)(2,1)} %v_hbm.1, bf16[512,256]{1,0:T(8,128)(2,1)} %g_hbm.1, s32[32]{0:T(128)} %len_ref.1), custom_call_target="tpu_custom_call" | custom-call | tf_op jit(solution)/shard_map/pallas_call | solution.py:449
  60.9 2.3 %shard_map.85 = (bf16[512,256]{1,0:T(8,128)(2,1)}, bf16[512,256]{1,0:T(8,128)(2,1)}, bf16[512,512]{1,0:T(8,128)(2,1)}, bf16[512,512]{1,0:T(8,128)(2,1)}) custom-call(bf16[512,256]{1,0:T(8,128)(2,1)} %get-tuple-element.7.o_raw, bf16[512,256]{1,0:T(8,128)(2,1)} %get-tuple-element.8.dq_raw, bf16[2,4,512,128]{3,2,1,0:T(8,128)(2,1)} %get-tuple-element.9.kvg_raw), custom_call_target="tpu_custom_call" | custom-call | tf_op jit(solution)/shard_map/pallas_call | solution.py:492

commit v5 on v4

--- a/solution.py
+++ b/solution.py
@@ -17,7 +17,7 @@
 CH = 256
 RB = 128
 QUART = 128
-NSUB = 2
+NSUB = 1
 SUB = QUART // NSUB
 STRAIGHT = (3, 4)
 NEG = -1e30
@@ -436,7 +436,7 @@
         cp.wait()
 
 
-N_SEND = 106
+N_SEND = 90
 
 
 def solution(mesh):

time: 63.9 us -> 64.6 us (1.011)
  Pallas kernels: 62.5 us -> 63.4 us
    pallas_call x1, Pallas kernels: 60.3 us -> 61.2 us  [per_device(): pl.pallas_call(functools.partial(kernel, n_ctx, doc_lengths.shape[0]), ou...]
where the time goes in v5:
time: 64.6 us; the launch traced here: 64.2 us
  Pallas kernels  63.4 us (98%)
  between operations  0.8 us (1%)
    pallas_call x1, Pallas kernels, per_device(): pl.pallas_call(functools.partial(kernel, n_ctx, doc_lengths.shape[0]), ou...  61.2 us
    pallas_call x1, Pallas kernels, per_device(): pl.pallas_call(place_outputs, out_shape=shapes, in_specs=[hbm] * 3, out_s...  2.25 us

profile of v5, /device:TPU:7, one launch (start us, length us, event | category | flops | bytes accessed | tf_op | source)
XLA Modules:
  0.0 64.2 jit_solution(9601450178341789241)
XLA Ops:
  0.6 61.2 %shard_map.84 = (bf16[512,256]{1,0:T(8,128)(2,1)}, bf16[512,256]{1,0:T(8,128)(2,1)}, bf16[2,4,512,128]{3,2,1,0:T(8,128)(2,1)}) custom-call(bf16[512,256]{1,0:T(8,128)(2,1)} %q_hbm.1, bf16[512,512]{1,0:T(8,128)(2,1)} %k_hbm.1, bf16[512,512]{1,0:T(8,128)(2,1)} %v_hbm.1, bf16[512,256]{1,0:T(8,128)(2,1)} %g_hbm.1, s32[32]{0:T(128)} %len_ref.1), custom_call_target="tpu_custom_call" | custom-call | tf_op jit(solution)/shard_map/pallas_call | solution.py:449
  61.8 2.3 %shard_map.85 = (bf16[512,256]{1,0:T(8,128)(2,1)}, bf16[512,256]{1,0:T(8,128)(2,1)}, bf16[512,512]{1,0:T(8,128)(2,1)}, bf16[512,512]{1,0:T(8,128)(2,1)}) custom-call(bf16[512,256]{1,0:T(8,128)(2,1)} %get-tuple-element.7.o_raw, bf16[512,256]{1,0:T(8,128)(2,1)} %get-tuple-element.8.dq_raw, bf16[2,4,512,128]{3,2,1,0:T(8,128)(2,1)} %get-tuple-element.9.kvg_raw), custom_call_target="tpu_custom_call" | custom-call | tf_op jit(solution)/shard_map/pallas_call | solution.py:492

commit v6 on v4

--- a/solution.py
+++ b/solution.py
@@ -38,7 +38,7 @@
 
 def kernel(n_ctx, ndoc, q_hbm, k_hbm, v_hbm, g_hbm, len_ref, o_ref, dq_ref, kvg_ref,
            q_in, g_in, kv, qt, gt, kvt, vtr, kx, sbuf, probs, dprob, acc, ot, dqt, gs, qs, ds,
-           term, cbuf, dbuf, hold, xsend, xbuf, zbuf, zsend, stage, o_v, dq_v, ksem, lsem, ssem, rsem):
+           term, cbuf, dbuf, hold, xsend, xbuf, zbuf, zsend, xs0, xr0, zdiag, stage, o_v, dq_v, ksem, lsem, ssem, rsem):
     c = lax.axis_index("ctx")
     t = lax.axis_index("tp")
     half_ctx = n_ctx // 2
@@ -58,6 +58,8 @@
     y_next = place(c, (y + 1) % 4, xl, core)
     y_prev = place(c, (y + 3) % 4, xl, core)
     x_diag = place(c, y, 1 - xl, 1 - core)
+    z_next_x = place((c + 1) % n_ctx, y, 1 - xl, core)
+    z_prev_x = place((c + n_ctx - 1) % n_ctx, y, 1 - xl, core)
     y_next_o = place(c, (y + 1) % 4, xl, 1 - core)
     y_prev_o = place(c, (y + 3) % 4, xl, 1 - core)
 
@@ -79,7 +81,7 @@
 
     barrier = pltpu.get_barrier_semaphore()
     peers = (x_peer, c_peer, y_next, y_prev, x_diag, y_next_o, y_prev_o)
-    for dev, ok in ((z_next, c < n_ctx - 1), (z_prev, c > 0)):
+    for dev, ok in ((z_next, c < n_ctx - 1), (z_prev, c > 0), (z_next_x, c < n_ctx - 1), (z_prev_x, c > 0)):
         @pl.when(ok)
         def _(dev=dev):
             pl.semaphore_signal(barrier, inc=1, device_id=dev, device_id_type=MESH)
@@ -88,7 +90,7 @@
         pl.semaphore_signal(barrier, inc=1, device_id=dev, device_id_type=MESH)
     for cp in loads[2:]:
         cp.wait()
-    pl.semaphore_wait(barrier, len(peers) + jnp.minimum(c, 1) + jnp.minimum(n_ctx - 1 - c, 1))
+    pl.semaphore_wait(barrier, len(peers) + 2 * jnp.minimum(c, 1) + 2 * jnp.minimum(n_ctx - 1 - c, 1))
 
     sent = []
 
@@ -300,6 +302,50 @@
             hold[s, j] = term[s, j, my_rows].astype(F32) + cbuf[s, j, mine].astype(F32)
 
 
+    def fold_c_last():
+        for j in (1, 0):
+            bc[0, j].wait_recv()
+            xs0[j] = (term[0, j, half_rows].astype(F32) + cbuf[0, j].astype(F32)).astype(BF)
+            bx[0, j] = send(xs0.at[j], xr0.at[j], x_peer)
+
+    def settle_last(j, at, arrived, rows):
+        total = xs0[j, at].astype(F32) + xr0[j, at].astype(F32) + arrived.astype(F32)
+        stage[j, y, rows] = total.astype(BF)
+
+    def finish_last():
+        coming = c < n_ctx - 1
+        for j in (1, 0):
+            bx[0, j].wait_recv()
+            for k in range(NSUB):
+                rows = slice(k * SUB, (k + 1) * SUB)
+
+                @pl.when(coming)
+                def _():
+                    bz[1, j, k].wait_recv()
+
+                @pl.when(c == n_ctx - 1)
+                def _():
+                    zbuf[0, j, rows] = jnp.zeros((SUB, HD), BF)
+
+                at = pl.ds(pl.multiple_of(xl * QUART + k * SUB, SUB), SUB)
+                settle_last(j, at, zbuf[0, j, rows], sub_rows[k])
+            piece = stage.at[j, y, my_rows]
+            aup[j] = send(piece, piece, y_next)
+            adn[j] = send(piece, piece, y_prev)
+        for j in (1, 0):
+            @pl.when(coming)
+            def _():
+                bd[j].wait_recv()
+
+            @pl.when(c == n_ctx - 1)
+            def _():
+                zdiag[j] = jnp.zeros((QUART, HD), BF)
+
+            settle_last(j, other, zdiag[j], other_rows)
+            piece = stage.at[j, y, other_rows]
+            xup[j] = send(piece, piece, y_next)
+            xdn[j] = send(piece, piece, y_prev)
+
     def fold_x(s):
         for j in (1, 0):
             if s in STRAIGHT:
@@ -325,21 +371,13 @@
                         zbuf[s, j, rows] = jnp.zeros((SUB, HD), BF)
 
                     total = total + zbuf[s, j, rows].astype(F32)
-                if s > 0:
-                    zsend[s, j, rows] = total.astype(BF)
-                    bz[s, j, k] = send(zsend.at[s, j, rows], zbuf.at[s - 1, j, rows], z_prev, c >= s)
-                else:
-                    stage[j, y, sub_rows[k]] = total.astype(BF)
-            if s == 0:
-                spread(j)
-
-    ax, aup, adn, xup, xdn = {}, {}, {}, {}, {}
-
-    def spread(j):
-        piece = stage.at[j, y, my_rows]
-        ax[j] = send(piece, piece, x_peer)
-        aup[j] = send(piece, piece, y_next)
-        adn[j] = send(piece, piece, y_prev)
+                zsend[s, j, rows] = total.astype(BF)
+                bz[s, j, k] = send(zsend.at[s, j, rows], zbuf.at[s - 1, j, rows], z_prev, c >= s)
+        if s == 1:
+            for j in (1, 0):
+                bd[j] = send(zsend.at[1, j], zdiag.at[j], z_prev_x, c >= 1)
+
+    aup, adn, xup, xdn, bd = {}, {}, {}, {}, {}
 
     kept = []
 
@@ -359,7 +397,7 @@
     backward(0)
     fold_x(3)
     fold_c(1)
-    fold_c(0)
+    fold_c_last()
     for h in range(2):
         o_v[:, h * HD:(h + 1) * HD] = ot[:, h * BLK:(h + 1) * BLK].T
     keep(o_v, o_ref)
@@ -370,7 +408,7 @@
     second_part = len(sent)
     fold_x(1)
     settle(second_part)
-    fold_x(0)
+    finish_last()
 
     below = (y + 3) % 4
     above = (y + 1) % 4
@@ -396,10 +434,6 @@
         keep(piece, out)
 
     for j in (1, 0):
-        ax[j].wait_recv()
-        piece = stage.at[j, y, other_rows]
-        xup[j] = send(piece, piece, y_next)
-        xdn[j] = send(piece, piece, y_prev)
         share(j, y)
     for j in (1, 0):
         aup[j].wait_recv()
@@ -477,6 +511,9 @@
                 pltpu.VMEM((steps, 2, QUART, HD), BF),
                 pltpu.VMEM((REACH, 2, QUART, HD), BF),
                 pltpu.VMEM((steps, 2, QUART, HD), BF),
+                pltpu.VMEM((2, 256, HD), BF),
+                pltpu.VMEM((2, 256, HD), BF),
+                pltpu.VMEM((2, QUART, HD), BF),
                 pltpu.VMEM((2, KVH, BLK, HD), BF),
                 pltpu.VMEM((BLK, 256), BF),
                 pltpu.VMEM((BLK, 256), BF),

time: 63.9 us -> 62.6 us (0.980)
  Pallas kernels: 62.5 us -> 61.4 us
    pallas_call x1, Pallas kernels: 60.3 us -> 59.1 us  [per_device(): pl.pallas_call(functools.partial(kernel, n_ctx, doc_lengths.shape[0]), ou...]
where the time goes in v6:
time: 62.6 us; the launch traced here: 62.2 us
  Pallas kernels  61.4 us (98%)
  between operations  0.8 us (1%)
    pallas_call x1, Pallas kernels, per_device(): pl.pallas_call(functools.partial(kernel, n_ctx, doc_lengths.shape[0]), ou...  59.1 us
    pallas_call x1, Pallas kernels, per_device(): pl.pallas_call(place_outputs, out_shape=shapes, in_specs=[hbm] * 3, out_s...  2.25 us

profile of v6, /device:TPU:7, one launch (start us, length us, event | category | flops | bytes accessed | tf_op | source)
XLA Modules:
  0.0 62.2 jit_solution(12340693309183616967)
XLA Ops:
  0.6 59.1 %shard_map.84 = (bf16[512,256]{1,0:T(8,128)(2,1)}, bf16[512,256]{1,0:T(8,128)(2,1)}, bf16[2,4,512,128]{3,2,1,0:T(8,128)(2,1)}) custom-call(bf16[512,256]{1,0:T(8,128)(2,1)} %q_hbm.1, bf16[512,512]{1,0:T(8,128)(2,1)} %k_hbm.1, bf16[512,512]{1,0:T(8,128)(2,1)} %v_hbm.1, bf16[512,256]{1,0:T(8,128)(2,1)} %g_hbm.1, s32[32]{0:T(128)} %len_ref.1), custom_call_target="tpu_custom_call" | custom-call | tf_op jit(solution)/shard_map/pallas_call | solution.py:483
  59.8 2.3 %shard_map.85 = (bf16[512,256]{1,0:T(8,128)(2,1)}, bf16[512,256]{1,0:T(8,128)(2,1)}, bf16[512,512]{1,0:T(8,128)(2,1)}, bf16[512,512]{1,0:T(8,128)(2,1)}) custom-call(bf16[512,256]{1,0:T(8,128)(2,1)} %get-tuple-element.7.o_raw, bf16[512,256]{1,0:T(8,128)(2,1)} %get-tuple-element.8.dq_raw, bf16[2,4,512,128]{3,2,1,0:T(8,128)(2,1)} %get-tuple-element.9.kvg_raw), custom_call_target="tpu_custom_call" | custom-call | tf_op jit(solution)/shard_map/pallas_call | solution.py:529

commit v7 on v6

--- a/solution.py
+++ b/solution.py
@@ -67,6 +67,7 @@
     my_half = pl.multiple_of(core * 256, 256)
     my_rows = pl.ds(pl.multiple_of(core * 256 + xl * QUART, QUART), QUART)
     sub_rows = [pl.ds(pl.multiple_of(core * 256 + xl * QUART + k * SUB, SUB), SUB) for k in range(NSUB)]
+    other_rows = pl.ds(pl.multiple_of(core * 256 + (1 - xl) * QUART, QUART), QUART)
     half_rows = pl.ds(my_half, 256)
     peer_half = pl.ds(pl.multiple_of((1 - core) * 256, 256), 256)
 
@@ -210,35 +211,49 @@
                 if s < REACH:
                     zc[s + 1, j, k] = send(kv.at[s, j, sub_rows[k]], kv.at[s + 1, j, sub_rows[k]], z_next,
                                            (c >= s) & (c < n_ctx - 1))
-            piece = kv.at[s, j, my_rows]
-            xc[s, j] = send(piece, piece, x_peer)
-            if s == REACH:
-                dc[s, j] = send(piece, piece, x_diag)
-                cc[s, j] = send(piece, piece, c_peer)
+            if s < REACH:
+                piece = kv.at[s, j, my_rows]
+                xc[s, j] = send(piece, piece, x_peer)
+            else:
+                @pl.when(c >= s)
+                def _():
+                    dc[s, j].wait_recv()
+
+                @pl.when(c < s)
+                def _():
+                    kv[s, j, other_rows] = jnp.zeros((QUART, HD), BF)
+
+                cc[s, j] = send(kv.at[s, j, half_rows], kv.at[s, j, half_rows], c_peer)
+        if s == REACH - 1:
+            for j in range(2):
+                dc[s + 1, j] = send(kv.at[s, j, my_rows], kv.at[s + 1, j, my_rows], z_next_x,
+                                    (c >= s) & (c < n_ctx - 1))
 
     def take_x(s):
         for j in range(2):
             xc[s, j].wait_recv()
-            if s < REACH:
-                cc[s, j] = send(kv.at[s, j, half_rows], kv.at[s, j, half_rows], c_peer)
+            cc[s, j] = send(kv.at[s, j, half_rows], kv.at[s, j, half_rows], c_peer)
 
     def take_c(s):
         for j in range(2):
             cc[s, j].wait_recv()
-            if s == REACH:
-                dc[s, j].wait_recv()
-
+
+    forward(0)
     take_z(1)
-    for s in range(1, REACH + 1):
-        if s < REACH:
-            take_z(s + 1)
-            take_x(s)
-        if s > 1:
-            take_c(s - 1)
-        forward(s - 1)
-    take_x(REACH)
-    take_c(REACH)
-    forward(REACH)
+    take_z(2)
+    take_x(1)
+    take_z(3)
+    take_x(2)
+    take_c(1)
+    forward(1)
+    take_x(3)
+    take_c(2)
+    forward(2)
+    take_z(4)
+    take_c(3)
+    forward(3)
+    take_c(4)
+    forward(4)
 
     inv, delta = [], []
     for i in range(nch):
@@ -470,7 +485,7 @@
         cp.wait()
 
 
-N_SEND = 106
+N_SEND = 104
 
 
 def solution(mesh):

time: 62.6 us -> 62.1 us (level)
  no operation moved by 1% of the time
where the time goes in v7:
time: 62.1 us; the launch traced here: 61.9 us
  Pallas kernels  61.1 us (98%)
  between operations  0.8 us (1%)
    pallas_call x1, Pallas kernels, per_device(): pl.pallas_call(functools.partial(kernel, n_ctx, doc_lengths.shape[0]), ou...  58.9 us
    pallas_call x1, Pallas kernels, per_device(): pl.pallas_call(place_outputs, out_shape=shapes, in_specs=[hbm] * 3, out_s...  2.25 us

profile of v7, /device:TPU:7, one launch (start us, length us, event | category | flops | bytes accessed | tf_op | source)
XLA Modules:
  0.0 61.9 jit_solution(15082791337650855389)
XLA Ops:
  0.6 58.9 %shard_map.84 = (bf16[512,256]{1,0:T(8,128)(2,1)}, bf16[512,256]{1,0:T(8,128)(2,1)}, bf16[2,4,512,128]{3,2,1,0:T(8,128)(2,1)}) custom-call(bf16[512,256]{1,0:T(8,128)(2,1)} %q_hbm.1, bf16[512,512]{1,0:T(8,128)(2,1)} %k_hbm.1, bf16[512,512]{1,0:T(8,128)(2,1)} %v_hbm.1, bf16[512,256]{1,0:T(8,128)(2,1)} %g_hbm.1, s32[32]{0:T(128)} %len_ref.1), custom_call_target="tpu_custom_call" | custom-call | tf_op jit(solution)/shard_map/pallas_call | solution.py:498
  59.5 2.3 %shard_map.85 = (bf16[512,256]{1,0:T(8,128)(2,1)}, bf16[512,256]{1,0:T(8,128)(2,1)}, bf16[512,512]{1,0:T(8,128)(2,1)}, bf16[512,512]{1,0:T(8,128)(2,1)}) custom-call(bf16[512,256]{1,0:T(8,128)(2,1)} %get-tuple-element.7.o_raw, bf16[512,256]{1,0:T(8,128)(2,1)} %get-tuple-element.8.dq_raw, bf16[2,4,512,128]{3,2,1,0:T(8,128)(2,1)} %get-tuple-element.9.kvg_raw), custom_call_target="tpu_custom_call" | custom-call | tf_op jit(solution)/shard_map/pallas_call | solution.py:544

commit v8 on v7

--- a/solution.py
+++ b/solution.py
@@ -17,7 +17,7 @@
 CH = 256
 RB = 128
 QUART = 128
-NSUB = 2
+NSUB = 4
 SUB = QUART // NSUB
 STRAIGHT = (3, 4)
 NEG = -1e30
@@ -485,7 +485,7 @@
         cp.wait()
 
 
-N_SEND = 104
+N_SEND = 136
 
 
 def solution(mesh):

time: 62.1 us -> 62.1 us (level)
  no operation moved by 1% of the time
where the time goes in v8:
time: 62.1 us; the launch traced here: 61.9 us
  Pallas kernels  61.1 us (98%)
  between operations  0.8 us (1%)
    pallas_call x1, Pallas kernels, per_device(): pl.pallas_call(functools.partial(kernel, n_ctx, doc_lengths.shape[0]), ou...  58.9 us
    pallas_call x1, Pallas kernels, per_device(): pl.pallas_call(place_outputs, out_shape=shapes, in_specs=[hbm] * 3, out_s...  2.25 us

profile of v8, /device:TPU:7, one launch (start us, length us, event | category | flops | bytes accessed | tf_op | source)
XLA Modules:
  0.0 61.9 jit_solution(4935763821060541404)
XLA Ops:
  0.6 58.9 %shard_map.84 = (bf16[512,256]{1,0:T(8,128)(2,1)}, bf16[512,256]{1,0:T(8,128)(2,1)}, bf16[2,4,512,128]{3,2,1,0:T(8,128)(2,1)}) custom-call(bf16[512,256]{1,0:T(8,128)(2,1)} %q_hbm.1, bf16[512,512]{1,0:T(8,128)(2,1)} %k_hbm.1, bf16[512,512]{1,0:T(8,128)(2,1)} %v_hbm.1, bf16[512,256]{1,0:T(8,128)(2,1)} %g_hbm.1, s32[32]{0:T(128)} %len_ref.1), custom_call_target="tpu_custom_call" | custom-call | tf_op jit(solution)/shard_map/pallas_call | solution.py:498
  59.5 2.3 %shard_map.85 = (bf16[512,256]{1,0:T(8,128)(2,1)}, bf16[512,256]{1,0:T(8,128)(2,1)}, bf16[512,512]{1,0:T(8,128)(2,1)}, bf16[512,512]{1,0:T(8,128)(2,1)}) custom-call(bf16[512,256]{1,0:T(8,128)(2,1)} %get-tuple-element.7.o_raw, bf16[512,256]{1,0:T(8,128)(2,1)} %get-tuple-element.8.dq_raw, bf16[2,4,512,128]{3,2,1,0:T(8,128)(2,1)} %get-tuple-element.9.kvg_raw), custom_call_target="tpu_custom_call" | custom-call | tf_op jit(solution)/shard_map/pallas_call | solution.py:544

commit v9 on v7

--- a/solution.py
+++ b/solution.py
@@ -476,9 +476,9 @@
             i = len(fetch)
             fetch.append(pltpu.make_async_copy(kvg_raw.at[j, g], kvg_v.at[j, g], isem.at[i]))
             store.append(pltpu.make_async_copy(kvg_v.at[j, g], out.at[:, g * HD:(g + 1) * HD], osem.at[i]))
-    for cp in fetch:
+    for cp in fetch[2:] + fetch[:2]:
         cp.start()
-    for get, put in zip(fetch, store):
+    for get, put in zip(fetch[2:] + fetch[:2], store[2:] + store[:2]):
         get.wait()
         put.start()
     for cp in store:

time: 62.1 us -> 62.2 us (level)
  no operation moved by 1% of the time
where the time goes in v9:
time: 62.2 us; the launch traced here: 62 us
  Pallas kernels  61.2 us (98%)
  between operations  0.8 us (1%)
    pallas_call x1, Pallas kernels, per_device(): pl.pallas_call(functools.partial(kernel, n_ctx, doc_lengths.shape[0]), ou...  58.9 us
    pallas_call x1, Pallas kernels, per_device(): pl.pallas_call(place_outputs, out_shape=shapes, in_specs=[hbm] * 3, out_s...  2.35 us

profile of v9, /device:TPU:7, one launch (start us, length us, event | category | flops | bytes accessed | tf_op | source)
XLA Modules:
  0.0 62.0 jit_solution(5676391743955973648)
XLA Ops:
  0.6 58.9 %shard_map.84 = (bf16[512,256]{1,0:T(8,128)(2,1)}, bf16[512,256]{1,0:T(8,128)(2,1)}, bf16[2,4,512,128]{3,2,1,0:T(8,128)(2,1)}) custom-call(bf16[512,256]{1,0:T(8,128)(2,1)} %q_hbm.1, bf16[512,512]{1,0:T(8,128)(2,1)} %k_hbm.1, bf16[512,512]{1,0:T(8,128)(2,1)} %v_hbm.1, bf16[512,256]{1,0:T(8,128)(2,1)} %g_hbm.1, s32[32]{0:T(128)} %len_ref.1), custom_call_target="tpu_custom_call" | custom-call | tf_op jit(solution)/shard_map/pallas_call | solution.py:498
  59.5 2.3 %shard_map.85 = (bf16[512,256]{1,0:T(8,128)(2,1)}, bf16[512,256]{1,0:T(8,128)(2,1)}, bf16[512,512]{1,0:T(8,128)(2,1)}, bf16[512,512]{1,0:T(8,128)(2,1)}) custom-call(bf16[512,256]{1,0:T(8,128)(2,1)} %get-tuple-element.7.o_raw, bf16[512,256]{1,0:T(8,128)(2,1)} %get-tuple-element.8.dq_raw, bf16[2,4,512,128]{3,2,1,0:T(8,128)(2,1)} %get-tuple-element.9.kvg_raw), custom_call_target="tpu_custom_call" | custom-call | tf_op jit(solution)/shard_map/pallas_call | solution.py:544
